TPU v7x, 512 devices: a whole 4x4x16 slice. The times are simulated.
512 devices in a mesh: slab: 64 (over y_hi, z, core), head: 8 (over y_lo, x).
Axes of the slice: x: 4, y: 4 (y_hi: 2, y_lo: 2; y = y_hi * 2 + y_lo), z: 16, core: 2. Of those that a mesh axis runs over, the one named last changes fastest.
Arguments:
- q_vals: bfloat16 [51200, 3072], P(('slab', 'head')), may hold values from -72 to 72
- k_vals: bfloat16 [51200, 3072], P(('slab', 'head')), may hold values from -6 to 6
- v_vals: bfloat16 [51200, 3072], P(('slab', 'head')), may hold values from -6 to 6
- q_scale: bfloat16 [51200, 24], P(('slab', 'head')), may hold values from 0.25 to 2.5
- k_scale: bfloat16 [51200, 24], P(('slab', 'head')), may hold values from 0.25 to 2.5
- v_scale: bfloat16 [51200, 24], P(('slab', 'head')), may hold values from 0.25 to 2.5
- window: int32 [24, 3], replicated, may hold values from 0 to 2, as said below
Outputs:
- attended: bfloat16 [51200, 3072], P(('slab', 'head'))
Inputs may be any that keep to these rules, and one draw needn't show every extreme that they name: window[h, 0] and window[h, 1] are 0 or 1; window[h, 2] is 0, 1 or 2.
All inputs are finite; a program needn't handle non-finite values.
Results may differ from a plain program's by a relative error of at most 0.011.
Values may be sent and summed in bfloat16 or wider, within the bound.
No kernel may reach another device: no remote copies, remote signals or barrier semaphores. Data moves between devices by JAX's collectives and lax.ppermute only.
A program may use at most 64 MiB of HBM per device.

v0:
```python
import jax
import jax.numpy as jnp
from jax import lax
from jax.sharding import PartitionSpec as P

SF = 1
TILE_H = 5
TILE_W = 8
FRAME_W = 80


def extended_2(array, sides, width):
    for axis, dim in sides:
        devices, length = (lax.axis_size(axis), array.shape[dim])
        up = [(i, (i + 1) % devices) for i in range(devices - 1)]
        down = [(j, i) for i, j in up]
        last = lax.slice_in_dim(array, length - width, length, axis=dim)
        initial = lax.slice_in_dim(array, 0, width, axis=dim)
        before = lax.ppermute(last, axis, up)
        after = lax.ppermute(initial, axis, down)
        array = jnp.concatenate([before, array, after], axis=dim)
    return array


def dequant(vals, scales, local_heads, head_dim):
    rows = vals.shape[0]
    wide = (
        vals.reshape(rows, local_heads, head_dim).astype(jnp.float32)
        * scales.astype(jnp.float32)[:, :, None]
    )
    return wide.astype(jnp.bfloat16).reshape(rows, local_heads * head_dim)


def widen(stacked):
    depth = stacked.shape[0]
    return extended_2(stacked, (("slab", 0),), depth)


def per_device(q_vals, k_vals, v_vals, q_scale, k_scale, v_scale, window):
    groups = lax.axis_size("head")
    slabs = lax.axis_size("slab")
    heads_all = q_scale.shape[1]
    local_heads = heads_all // groups
    head_dim = q_vals.shape[1] // heads_all
    width = local_heads * head_dim
    q_got, k_got, v_got, qs_got, ks_got, vs_got = (
        lax.all_to_all(q_vals, "head", split_axis=1, concat_axis=0, tiled=True),
        lax.all_to_all(k_vals, "head", split_axis=1, concat_axis=0, tiled=True),
        lax.all_to_all(v_vals, "head", split_axis=1, concat_axis=0, tiled=True),
        lax.all_to_all(q_scale, "head", split_axis=1, concat_axis=0, tiled=True),
        lax.all_to_all(k_scale, "head", split_axis=1, concat_axis=0, tiled=True),
        lax.all_to_all(v_scale, "head", split_axis=1, concat_axis=0, tiled=True),
    )
    stacked = jnp.concatenate(
        [
            dequant(k_got, ks_got, local_heads, head_dim),
            dequant(v_got, vs_got, local_heads, head_dim),
        ],
        1,
    )
    extended = widen(stacked)
    queries = dequant(q_got, qs_got, local_heads, head_dim)
    slab_rows = queries.shape[0]
    frame = slab_rows // SF
    block = TILE_H * FRAME_W
    blocks = frame // block
    span = 2 * SF + 1
    places = jnp.arange(frame, dtype=jnp.int32)
    tile_row = places // FRAME_W // TILE_H
    tile_col = places % FRAME_W // TILE_W
    key_row = jnp.tile(tile_row, span)
    key_col = jnp.tile(tile_col, span)
    key_frame = jnp.repeat(jnp.arange(span, dtype=jnp.int32), frame)
    frame_gap = jnp.abs(key_frame - SF)
    head_base = lax.axis_index("head") * local_heads
    local_window = lax.dynamic_slice_in_dim(window, head_base, local_heads, 0)
    first_frame = lax.axis_index("slab") * SF - SF
    total_frames = slabs * SF
    scale = 1.0 / head_dim**0.5
    key_global = first_frame + 0 + key_frame
    inside = (key_global >= 0) & (key_global < total_frames)
    blocks_out = []
    for part_index in range(blocks):
        low = part_index * block
        row_gap = jnp.abs(tile_row[low : low + block][:, None] - key_row[None, :])
        col_gap = jnp.abs(tile_col[low : low + block][:, None] - key_col[None, :])
        heads_out = []
        for head in range(local_heads):
            q_block = queries[low : low + block, head * head_dim : (head + 1) * head_dim]
            k_block = extended[:, head * head_dim : (head + 1) * head_dim]
            v_block = extended[:, width + head * head_dim : width + (head + 1) * head_dim]
            scores = (
                jnp.einsum("qd,kd->qk", q_block, k_block, preferred_element_type=jnp.float32)
                * scale
            )
            allowed = (frame_gap <= local_window[head, 0])[None, :] & inside[None, :]
            allowed = (
                allowed & (row_gap <= local_window[head, 1]) & (col_gap <= local_window[head, 2])
            )
            masked = jnp.where(allowed, scores, -1e30)
            top = jnp.max(masked, axis=-1, keepdims=True)
            expd = jnp.exp(masked - top)
            probs = expd / jnp.sum(expd, axis=-1, keepdims=True)
            weights = probs.astype(jnp.bfloat16)
            result = jnp.dot(weights, v_block, preferred_element_type=jnp.float32)
            heads_out.append(result.astype(jnp.bfloat16))
        blocks_out.append(jnp.concatenate(heads_out, 1))
    frames_out = jnp.concatenate(blocks_out, 0)
    return lax.all_to_all(frames_out, "head", split_axis=0, concat_axis=1, tiled=True)


def solution(mesh):
    return jax.shard_map(
        per_device,
        mesh=mesh,
        in_specs=(
            P(("slab", "head"), None),
            P(("slab", "head"), None),
            P(("slab", "head"), None),
            P(("slab", "head"), None),
            P(("slab", "head"), None),
            P(("slab", "head"), None),
            P(),
        ),
        out_specs=P(("slab", "head"), None),
        check_vma=False,
    )
```

profile of v0, /device:TPU:1, one launch (start us, length us, event | category | flops | bytes accessed | tf_op | source)
XLA Modules:
  0.0 148.7 jit_solution(8456334361398652609)
XLA Ops:
  0.0 1.4 all_to_all.84
  1.4 5.9 %all-to-all-start.5 = ((bf16[100,8,3]{0,2,1:T(4,128)(2,1)}), bf16[100,8,3]{0,2,1:T(4,128)(2,1)S(1)}, u32[]{:S(2)}, u32[]{:S(2)}) async-start(bf16[100,8,3]{0,2,1:T(4,128)(2,1)} %all_to_all.84), calls=%async_computation.5 | async-start | bytes 16384 | tf_op jit(solution)/shard_map/all_to_all | solution.py:52
  7.2 1.3 all_to_all.80
  8.5 3.7 %all-to-all-done.5 = bf16[100,8,3]{0,2,1:T(4,128)(2,1)S(1)} async-done(((bf16[100,8,3]{0,2,1:T(4,128)(2,1)}), bf16[100,8,3]{0,2,1:T(4,128)(2,1)S(1)}, u32[]{:S(2)}, u32[]{:S(2)}) %all-to-all-start.5) | async-done | bytes 4832 | tf_op jit(solution)/shard_map/all_to_all | solution.py:52
  12.3 3.3 %all-to-all-start.3 = ((bf16[100,8,3]{0,2,1:T(4,128)(2,1)}), bf16[100,8,3]{0,2,1:T(4,128)(2,1)S(1)}, u32[]{:S(2)}, u32[]{:S(2)}) async-start(bf16[100,8,3]{0,2,1:T(4,128)(2,1)} %all_to_all.80), calls=%async_computation.3 | async-start | bytes 16384 | tf_op jit(solution)/shard_map/all_to_all | solution.py:51
  15.6 1.2 copy.29
  16.9 0.9 copy.21
  17.8 2.8 %all-to-all-done.3 = bf16[100,8,3]{0,2,1:T(4,128)(2,1)S(1)} async-done(((bf16[100,8,3]{0,2,1:T(4,128)(2,1)}), bf16[100,8,3]{0,2,1:T(4,128)(2,1)S(1)}, u32[]{:S(2)}, u32[]{:S(2)}) %all-to-all-start.3) | async-done | bytes 4832 | tf_op jit(solution)/shard_map/all_to_all | solution.py:51
  20.6 3.5 %all-to-all-start.2 = ((bf16[100,8,384]{2,0,1:T(8,128)(2,1)}), bf16[100,8,384]{2,0,1:T(8,128)(2,1)S(1)}, u32[]{:S(2)}, u32[]{:S(2)}) async-start(bf16[100,8,384]{2,0,1:T(8,128)(2,1)} %copy.21), calls=%async_computation.2 | async-start | bytes 1277952 | tf_op jit(solution)/shard_map/all_to_all | solution.py:48
  24.9 0.9 copy.24
  25.9 0.7 fusion.90
  26.6 1.2 fusion.71
  27.9 4.4 %all-to-all-done.2 = bf16[100,8,384]{2,0,1:T(8,128)(2,1)S(1)} async-done(((bf16[100,8,384]{2,0,1:T(8,128)(2,1)}), bf16[100,8,384]{2,0,1:T(8,128)(2,1)S(1)}, u32[]{:S(2)}, u32[]{:S(2)}) %all-to-all-start.2) | async-done | bytes 614432 | tf_op jit(solution)/shard_map/all_to_all | solution.py:48
  32.2 4.2 %all-to-all-start.4 = ((bf16[100,8,384]{2,0,1:T(8,128)(2,1)}), bf16[100,8,384]{2,0,1:T(8,128)(2,1)}, u32[]{:S(2)}, u32[]{:S(2)}) async-start(bf16[100,8,384]{2,0,1:T(8,128)(2,1)} %copy.24), calls=%async_computation.4 | async-start | bytes 1277952 | tf_op jit(solution)/shard_map/all_to_all | solution.py:49
  37.3 1.4 copy.26
  38.8 1.2 reshape.177
  40.0 4.6 %all-to-all-done.4 = bf16[100,8,384]{2,0,1:T(8,128)(2,1)} async-done(((bf16[100,8,384]{2,0,1:T(8,128)(2,1)}), bf16[100,8,384]{2,0,1:T(8,128)(2,1)}, u32[]{:S(2)}, u32[]{:S(2)}) %all-to-all-start.4) | async-done | bytes 614432 | tf_op jit(solution)/shard_map/all_to_all | solution.py:49
  44.6 3.3 %all-to-all-start.1 = ((bf16[100,8,3]{0,2,1:T(4,128)(2,1)}), bf16[100,8,3]{0,2,1:T(4,128)(2,1)S(1)}, u32[]{:S(2)}, u32[]{:S(2)}) async-start(bf16[100,8,3]{0,2,1:T(4,128)(2,1)} %all_to_all.76), calls=%async_computation.1 | async-start | bytes 16384 | tf_op jit(solution)/shard_map/all_to_all | solution.py:50
  47.9 1.2 convert_bitcast_fusion
  49.1 1.2 reshape.179
  50.3 2.3 %multiply_convert_fusion = (bf16[800,384]{1,0:T(8,128)(2,1)S(1)}, bf16[800,384]{1,0:T(8,128)(2,1)S(1)}) fusion(f32[800,384]{1,0:T(8,128)} %reshape.179, f32[800,384]{1,0:T(8,128)} %copy.26, f32[800,384]{1,0:T(8,128)} %reshape.177, f32[800,384]{1,0:T(8,128)S(1)} %copy.23), kind=kLoop, calls=%fused_computation.69 | loop fusion | flops 1228800 | bytes 6144000 | tf_op jit(solution)/shard_map/convert_element_type | solution.py:31
  52.6 1.1 pad_maximum_fusion.1
  53.8 10.8 %collective-permute-start.1 = (bf16[800,768]{1,0:T(8,128)(2,1)}, bf16[800,768]{1,0:T(8,128)(2,1)}, u32[]{:S(2)}, u32[]{:S(2)}) collective-permute-start(bf16[800,768]{1,0:T(8,128)(2,1)} %pad_maximum_fusion.1), channel_id=1, source_target_pairs={{8,0},{16,8},{24,16},{32,24},{40,32},{48,40},{56,48},{64,56},{72,6... | collective-permute-start | bytes 3686408 | tf_op jit(solution)/shard_map/ppermute | solution.py:20
  64.6 1.9 %collective-permute-start = (bf16[800,768]{1,0:T(8,128)(2,1)}, bf16[800,768]{1,0:T(8,128)(2,1)}, u32[]{:S(2)}, u32[]{:S(2)}) collective-permute-start(bf16[800,768]{1,0:T(8,128)(2,1)} %pad_maximum_fusion.1), channel_id=1, source_target_pairs={{0,8},{8,16},{16,24},{24,32},{32,40},{40,48},{48,56},{56,64},{64,7... | collective-permute-start | bytes 3686408 | tf_op jit(solution)/shard_map/ppermute | solution.py:19
  67.7 0.9 copy.18
  68.7 5.4 %all-to-all-start = ((bf16[100,8,384]{2,0,1:T(8,128)(2,1)}), bf16[100,8,384]{2,0,1:T(8,128)(2,1)S(1)}, u32[]{:S(2)}, u32[]{:S(2)}) async-start(bf16[100,8,384]{2,0,1:T(8,128)(2,1)} %copy.18), calls=%async_computation | async-start | bytes 1277952 | tf_op jit(solution)/shard_map/all_to_all | solution.py:47
  74.4 1.5 copy.20
  75.9 19.2 %all-to-all-done = bf16[100,8,384]{2,0,1:T(8,128)(2,1)S(1)} async-done(((bf16[100,8,384]{2,0,1:T(8,128)(2,1)}), bf16[100,8,384]{2,0,1:T(8,128)(2,1)S(1)}, u32[]{:S(2)}, u32[]{:S(2)}) %all-to-all-start) | async-done | bytes 614432 | tf_op jit(solution)/shard_map/all_to_all | solution.py:47
  95.2 1.2 reshape.175
  96.4 1.8 %multiply_convert_fusion.2 = bf16[800,384]{1,0:T(8,128)(2,1)S(1)} fusion(f32[800,384]{1,0:T(8,128)} %reshape.175, f32[800,384]{1,0:T(8,128)} %copy.20), kind=kLoop, calls=%fused_computation.71 | loop fusion | flops 614400 | bytes 3072000 | tf_op jit(solution)/shard_map/convert_element_type | solution.py:31
  98.1 2.7 %pad_maximum_fusion = bf16[2400,768]{1,0:T(8,128)(2,1)S(1)} fusion(bf16[800,768]{1,0:T(8,128)(2,1)} %collective-permute-done.1, bf16[800,384]{1,0:T(8,128)(2,1)S(1)} %get-tuple-element.30, bf16[800,384]{1,0:T(8,128)(2,1)S(1)} %get-tuple-element.31, bf16[800,768]{1,0:T(8,128)(2,1)} %collective-permute-done), kind=kLoop, calls=%fused_computation.52 | loop fusion | flops 14745600 | bytes 7372800 | tf_op jit(solution)/shard_map/concatenate | solution.py:21
  100.8 3.9 %fusion.93 = (f32[400]{0:T(512)S(1)}, f32[400,2400]{1,0:T(8,128)S(1)}) fusion(bf16[2400,768]{1,0:T(8,128)(2,1)S(1)} %pad_maximum_fusion, bf16[800,384]{1,0:T(8,128)(2,1)S(1)} %multiply_convert_fusion.2, s32[]{:T(128)} %bitcast.2, s32[2400]{0:T(1024)S(1)} %sub.237, s32[400]{0:T(512)S(1)} %get-tuple-element.34, s32[]{:T(128)} %bitcast.1, ...), kind=kOutput, calls=%fused_computation.141 | convolution fusion | flops 256319600 | bytes 4590152 | tf_op jit(solution)/shard_map/qd,kd->qk/dot_general | solution.py:93
  104.7 3.9 %fusion.96 = (f32[400]{0:T(512)S(1)}, f32[400,2400]{1,0:T(8,128)S(1)}) fusion(bf16[2400,768]{1,0:T(8,128)(2,1)S(1)} %pad_maximum_fusion, bf16[800,384]{1,0:T(8,128)(2,1)S(1)} %multiply_convert_fusion.2, s32[]{:T(128)} %bitcast.2, s32[2400]{0:T(1024)S(1)} %sub.237, s32[400]{0:T(512)S(1)} %get-tuple-element.35, s32[]{:T(128)} %bitcast.1, ...), kind=kOutput, calls=%fused_computation.144 | convolution fusion | flops 256319600 | bytes 4590152 | tf_op jit(solution)/shard_map/qd,kd->qk/dot_general | solution.py:93
  108.5 3.7 %fusion.91 = (f32[400]{0:T(512)S(1)}, f32[400,2400]{1,0:T(8,128)S(1)}) fusion(bf16[2400,768]{1,0:T(8,128)(2,1)S(1)} %pad_maximum_fusion, bf16[800,384]{1,0:T(8,128)(2,1)S(1)} %multiply_convert_fusion.2, s32[]{:T(128)} %bitcast.17, s32[2400]{0:T(1024)S(1)} %sub.237, s32[400]{0:T(512)S(1)} %get-tuple-element.34, s32[]{:T(128)} %bitcast.16, ...), kind=kOutput, calls=%fused_computation.139 | convolution fusion | flops 256319600 | bytes 4590152 | tf_op jit(solution)/shard_map/qd,kd->qk/dot_general | solution.py:93
  112.2 3.7 %fusion.94 = (f32[400]{0:T(512)S(1)}, f32[400,2400]{1,0:T(8,128)S(1)}) fusion(bf16[2400,768]{1,0:T(8,128)(2,1)S(1)} %pad_maximum_fusion, bf16[800,384]{1,0:T(8,128)(2,1)S(1)} %multiply_convert_fusion.2, s32[]{:T(128)} %bitcast.17, s32[2400]{0:T(1024)S(1)} %sub.237, s32[400]{0:T(512)S(1)} %get-tuple-element.35, s32[]{:T(128)} %bitcast.16, ...), kind=kOutput, calls=%fused_computation.142 | convolution fusion | flops 256319600 | bytes 4590152 | tf_op jit(solution)/shard_map/qd,kd->qk/dot_general | solution.py:93
  115.9 3.9 %fusion.92 = (f32[400]{0:T(512)S(1)}, f32[400,2400]{1,0:T(8,128)S(1)}) fusion(bf16[2400,768]{1,0:T(8,128)(2,1)S(1)} %pad_maximum_fusion, bf16[800,384]{1,0:T(8,128)(2,1)S(1)} %multiply_convert_fusion.2, s32[]{:T(128)} %bitcast.14, s32[2400]{0:T(1024)S(1)} %sub.237, s32[400]{0:T(512)S(1)} %get-tuple-element.34, s32[]{:T(128)} %bitcast.13, ...), kind=kOutput, calls=%fused_computation.140 | convolution fusion | flops 256319600 | bytes 4590152 | tf_op jit(solution)/shard_map/qd,kd->qk/dot_general | solution.py:93
  119.9 3.7 %fusion.95 = (f32[400]{0:T(512)S(1)}, f32[400,2400]{1,0:T(8,128)S(1)}) fusion(bf16[2400,768]{1,0:T(8,128)(2,1)S(1)} %pad_maximum_fusion, bf16[800,384]{1,0:T(8,128)(2,1)S(1)} %multiply_convert_fusion.2, s32[]{:T(128)} %bitcast.14, s32[2400]{0:T(1024)S(1)} %sub.237, s32[400]{0:T(512)S(1)} %get-tuple-element.35, s32[]{:T(128)} %bitcast.13, ...), kind=kOutput, calls=%fused_computation.143 | convolution fusion | flops 256319600 | bytes 4590152 | tf_op jit(solution)/shard_map/qd,kd->qk/dot_general | solution.py:93
  123.6 0.7 fusion.33
  124.3 0.8 fusion.44
  125.1 0.7 fusion.30
  125.8 0.8 fusion.47
  127.3 0.8 fusion.43
  128.1 0.7 fusion.35
  128.8 0.8 fusion.42
  130.3 0.8 fusion.45
  131.8 0.8 fusion.46
  132.8 14.8 %all_to_all.97 = bf16[8,100,384]{2,1,0:T(8,128)(2,1)S(1)} all-to-all(bf16[8,100,384]{2,1,0:T(8,128)(2,1)S(1)} %all_to_all.86), channel_id=1, replica_groups=mesh['slab'=64,'head'=8] {'head'}, dimensions={0} | all-to-all | bytes 1228800 | tf_op jit(solution)/shard_map/all_to_all | solution.py:109
  147.8 0.9 copy.31
  (51 shorter events, 5.7 us)
Async XLA Ops:
  0.0 25.8 %copy-start = (s32[24,3]{0,1:T(4,128)S(1)}, s32[24,3]{0,1:T(4,128)}, u32[]{:S(2)}) copy-start(s32[24,3]{0,1:T(4,128)} %param.13) | copy-start | bytes 868
  0.0 24.1 %copy-start.3 = (bf16[100,24]{0,1:T(8,128)(2,1)S(1)}, bf16[100,24]{0,1:T(8,128)(2,1)}, u32[]{:S(2)}) copy-start(bf16[100,24]{0,1:T(8,128)(2,1)} %param.10) | copy-start | bytes 14404
  0.0 24.8 %copy-start.1 = (bf16[100,3072]{1,0:T(8,128)(2,1)S(1)}, bf16[100,3072]{1,0:T(8,128)(2,1)}, u32[]{:S(2)}) copy-start(bf16[100,3072]{1,0:T(8,128)(2,1)} %param.9) | copy-start | bytes 1843204
  1.4 10.9 %all-to-all-start.5 = ((bf16[100,8,3]{0,2,1:T(4,128)(2,1)}), bf16[100,8,3]{0,2,1:T(4,128)(2,1)S(1)}, u32[]{:S(2)}, u32[]{:S(2)}) async-start(bf16[100,8,3]{0,2,1:T(4,128)(2,1)} %all_to_all.84), calls=%async_computation.5 | async-start | bytes 16384 | tf_op jit(solution)/shard_map/all_to_all | solution.py:52
  12.3 8.3 %all-to-all-start.3 = ((bf16[100,8,3]{0,2,1:T(4,128)(2,1)}), bf16[100,8,3]{0,2,1:T(4,128)(2,1)S(1)}, u32[]{:S(2)}, u32[]{:S(2)}) async-start(bf16[100,8,3]{0,2,1:T(4,128)(2,1)} %all_to_all.80), calls=%async_computation.3 | async-start | bytes 16384 | tf_op jit(solution)/shard_map/all_to_all | solution.py:51
  20.6 11.6 %all-to-all-start.2 = ((bf16[100,8,384]{2,0,1:T(8,128)(2,1)}), bf16[100,8,384]{2,0,1:T(8,128)(2,1)S(1)}, u32[]{:S(2)}, u32[]{:S(2)}) async-start(bf16[100,8,384]{2,0,1:T(8,128)(2,1)} %copy.21), calls=%async_computation.2 | async-start | bytes 1277952 | tf_op jit(solution)/shard_map/all_to_all | solution.py:48
  32.2 12.4 %all-to-all-start.4 = ((bf16[100,8,384]{2,0,1:T(8,128)(2,1)}), bf16[100,8,384]{2,0,1:T(8,128)(2,1)}, u32[]{:S(2)}, u32[]{:S(2)}) async-start(bf16[100,8,384]{2,0,1:T(8,128)(2,1)} %copy.24), calls=%async_computation.4 | async-start | bytes 1277952 | tf_op jit(solution)/shard_map/all_to_all | solution.py:49
  44.6 24.0 %all-to-all-start.1 = ((bf16[100,8,3]{0,2,1:T(4,128)(2,1)}), bf16[100,8,3]{0,2,1:T(4,128)(2,1)S(1)}, u32[]{:S(2)}, u32[]{:S(2)}) async-start(bf16[100,8,3]{0,2,1:T(4,128)(2,1)} %all_to_all.76), calls=%async_computation.1 | async-start | bytes 16384 | tf_op jit(solution)/shard_map/all_to_all | solution.py:50
  50.3 17.3 %copy-start.2 = (bf16[100,3072]{1,0:T(8,128)(2,1)S(1)}, bf16[100,3072]{1,0:T(8,128)(2,1)}, u32[]{:S(2)}) copy-start(bf16[100,3072]{1,0:T(8,128)(2,1)} %param.7) | copy-start | bytes 1843204
  53.8 44.3 %collective-permute-start.1 = (bf16[800,768]{1,0:T(8,128)(2,1)}, bf16[800,768]{1,0:T(8,128)(2,1)}, u32[]{:S(2)}, u32[]{:S(2)}) collective-permute-start(bf16[800,768]{1,0:T(8,128)(2,1)} %pad_maximum_fusion.1), channel_id=1, source_target_pairs={{8,0},{16,8},{24,16},{32,24},{40,32},{48,40},{56,48},{64,56},{72,6... | collective-permute-start | bytes 3686408 | tf_op jit(solution)/shard_map/ppermute | solution.py:20
  64.6 33.5 %collective-permute-start = (bf16[800,768]{1,0:T(8,128)(2,1)}, bf16[800,768]{1,0:T(8,128)(2,1)}, u32[]{:S(2)}, u32[]{:S(2)}) collective-permute-start(bf16[800,768]{1,0:T(8,128)(2,1)} %pad_maximum_fusion.1), channel_id=1, source_target_pairs={{0,8},{8,16},{16,24},{24,32},{32,40},{40,48},{48,56},{56,64},{64,7... | collective-permute-start | bytes 3686408 | tf_op jit(solution)/shard_map/ppermute | solution.py:19
  68.7 26.4 %all-to-all-start = ((bf16[100,8,384]{2,0,1:T(8,128)(2,1)}), bf16[100,8,384]{2,0,1:T(8,128)(2,1)S(1)}, u32[]{:S(2)}, u32[]{:S(2)}) async-start(bf16[100,8,384]{2,0,1:T(8,128)(2,1)} %copy.18), calls=%async_computation | async-start | bytes 1277952 | tf_op jit(solution)/shard_map/all_to_all | solution.py:47
where the time goes:
time: 150 us; the launch traced here: 149 us
  starting transfers between devices  38.4 us (26%)
  waiting for transfers between devices  34.8 us (23%)
  matrix products  27.8 us (19%)
  local copies, waits for them, and re-layouts  17.4 us (12%)
  other arithmetic  15.3 us (10%)
  blocking collectives  14.8 us (10%)
    dot_general x6, matrix products, per_device(): jnp.einsum('qd,kd->qk', q_block, k_block, preferred_element_type=jnp.floa...  22.8 us
    all_to_all x1, waiting for transfers between devices, per_device(): lax.all_to_all(q_vals, 'head', split_axis=1, concat_axis=0, tiled=True)  19.2 us
    all_to_all x1, blocking collectives, per_device(): lax.all_to_all(frames_out, 'head', split_axis=0, concat_axis=1, tiled=True)  14.8 us
    ppermute x1, starting transfers between devices, extended_2(): after = lax.ppermute(initial, axis, down)  10.8 us
    all_to_all x1, starting transfers between devices, per_device(): lax.all_to_all(v_scale, 'head', split_axis=1, concat_axis=0, tiled=True)  5.86 us
    all_to_all x1, starting transfers between devices, per_device(): lax.all_to_all(q_vals, 'head', split_axis=1, concat_axis=0, tiled=True)  5.35 us
    dot_general x6, matrix products, per_device(): result = jnp.dot(weights, v_block, preferred_element_type=jnp.float32)  5 us
    all_to_all x1, waiting for transfers between devices, per_device(): lax.all_to_all(v_vals, 'head', split_axis=1, concat_axis=0, tiled=True)  4.64 us
  transfers between devices with their start and end apart: 8, of which 5 were waited for; matrix products, arithmetic and copies ran while one was open for 14% of the time, Pallas kernels for 0%

commit v1 on v0

v1 whole, which is shorter than its diff:
```python
import functools

import jax
import jax.numpy as jnp
from jax import lax
from jax.experimental import pallas as pl
from jax.experimental.pallas import tpu as pltpu
from jax.sharding import PartitionSpec as P

TILE_H = 5
TILE_W = 8
FRAME_W = 80
HEAD_DIM = 128
MASKED = -1e30


def geometry(tokens):
    rows = tokens // FRAME_W
    return rows, FRAME_W // TILE_W, rows * TILE_W


def padded(rows):
    return -(-rows // 8) * 8


def pack_kernel(flip_ref, *refs, groups):
    count = (len(refs) - 1) // 2
    out_ref = refs[-1]
    rows = refs[0].shape[0]
    width = refs[0].shape[1] // groups
    heads = width // HEAD_DIM
    slot_rows = out_ref.shape[1]
    blank = jnp.zeros((slot_rows - rows, HEAD_DIM), jnp.float32)
    for at in range(count):
        vals_ref, scale_ref = refs[2 * at], refs[2 * at + 1]
        scales = scale_ref[...].astype(jnp.float32)
        for group in range(groups):
            slot = group ^ flip_ref[0]
            for head in range(heads):
                index = group * heads + head
                vals = vals_ref[:, index * HEAD_DIM : (index + 1) * HEAD_DIM]
                wide = vals.astype(jnp.float32) * scales[:, index : index + 1]
                if slot_rows > rows:
                    wide = jnp.concatenate([wide, blank], 0)
                low = at * width + head * HEAD_DIM
                out_ref[slot, :, low : low + HEAD_DIM] = wide.astype(jnp.bfloat16)


def pack(flip, pairs, groups):
    rows, full = pairs[0][0].shape
    width = full // groups
    vmem = pl.BlockSpec(memory_space=pltpu.VMEM)
    return pl.pallas_call(
        functools.partial(pack_kernel, groups=groups),
        out_shape=jax.ShapeDtypeStruct(
            (groups, padded(rows), width * len(pairs)), jnp.bfloat16
        ),
        in_specs=[pl.BlockSpec(memory_space=pltpu.SMEM)] + [vmem] * (2 * len(pairs)),
        out_specs=vmem,
        compiler_params=pltpu.CompilerParams(vmem_limit_bytes=32 * 2**20),
        cost_estimate=pl.CostEstimate(
            flops=rows * full * len(pairs),
            bytes_accessed=4 * rows * full * len(pairs),
            transcendentals=0,
        ),
    )(flip, *[ref for pair in pairs for ref in pair])


def unpack_kernel(flip_ref, in_ref, out_ref):
    groups, _, width = in_ref.shape
    rows = out_ref.shape[0]
    for group in range(groups):
        slot = in_ref[group ^ flip_ref[0]]
        out_ref[:, group * width : (group + 1) * width] = slot[:rows]


def unpack(flip, slots, rows):
    groups, _, width = slots.shape
    vmem = pl.BlockSpec(memory_space=pltpu.VMEM)
    return pl.pallas_call(
        unpack_kernel,
        out_shape=jax.ShapeDtypeStruct((rows, groups * width), jnp.bfloat16),
        in_specs=[pl.BlockSpec(memory_space=pltpu.SMEM), vmem],
        out_specs=vmem,
        compiler_params=pltpu.CompilerParams(vmem_limit_bytes=32 * 2**20),
    )(flip, slots)


def by_columns(slots_ref, lin_ref, chunk):
    slots = slots_ref.shape[0]
    rows, cols, _ = geometry(slots * chunk)
    for slot in range(slots):
        part = slots_ref[slot].astype(jnp.float32)
        lin_ref[slot * chunk : slot * chunk + part.shape[0], :] = part
    for col in range(cols):
        pieces = []
        for row in range(rows):
            low = row * FRAME_W + col * TILE_W
            pieces.append(lin_ref[low : low + TILE_W, :])
        yield col, jnp.concatenate(pieces, 0)


def attend_kernel(meta_ref, q_ref, *refs, chunk, block_cols, reach):
    keys_in, values_in = refs[0:3], refs[3:6]
    out_ref, lin_ref, qs_ref, ks_ref, vs_ref, lin_out_ref = refs[6:]
    slots, slot_rows, _ = q_ref.shape
    rows, cols, strip = geometry(slots * chunk)
    half = strip * TILE_H // rows
    classes = rows // TILE_H
    span = len(keys_in)
    head = pl.program_id(0)
    reach_frame = meta_ref[3 * head]
    reach_row = meta_ref[3 * head + 1]
    reach_col = meta_ref[3 * head + 2]
    first = jnp.where(reach_frame >= 1, meta_ref[meta_ref.shape[0] - 2], 1)
    last = jnp.where(reach_frame >= 1, meta_ref[meta_ref.shape[0] - 1], 1)

    @pl.when(head == 0)
    def _():
        vs_ref[:, HEAD_DIM:] = jnp.ones(
            (vs_ref.shape[0], vs_ref.shape[1] - HEAD_DIM), vs_ref.dtype
        )

    for col, part in by_columns(q_ref, lin_ref, chunk):
        qs_ref[col * strip : (col + 1) * strip, :] = part.astype(jnp.bfloat16)
    for frame in range(span):
        for col, part in by_columns(keys_in[frame], lin_ref, chunk):
            low = (col * span + frame) * strip
            ks_ref[low : low + strip, :] = part.astype(jnp.bfloat16)
        for col, part in by_columns(values_in[frame], lin_ref, chunk):
            low = (col * span + frame) * strip
            vs_ref[low : low + strip, :HEAD_DIM] = part.astype(jnp.bfloat16)

    scale = 1.4426950408889634 / HEAD_DIM**0.5
    for start in range(0, cols, block_cols):
        low_col, high_col = max(0, start - reach), min(cols, start + block_cols + reach)
        keys = (high_col - low_col) * span * strip
        at = lax.broadcasted_iota(jnp.int32, (1, keys), 1).astype(jnp.float32)
        key_col = jnp.floor((at + 0.5) * (1.0 / (span * strip)))
        rest = at - key_col * (span * strip)
        key_frame = jnp.floor((rest + 0.5) * (1.0 / strip))
        rest = rest - key_frame * strip
        key_row = jnp.floor((rest + 0.5) * (1.0 / half))
        frame_ok = (key_frame >= first.astype(jnp.float32)) & (
            key_frame <= last.astype(jnp.float32)
        )
        q_block = qs_ref[start * strip : (start + block_cols) * strip, :]
        key_rows = slice(low_col * span * strip, high_col * span * strip)
        scores = lax.dot_general(
            q_block,
            ks_ref[key_rows, :],
            (((1,), (1,)), ((), ())),
            preferred_element_type=jnp.float32,
        )
        weights = []
        for col in range(start, start + block_cols):
            col_ok = frame_ok & (
                jnp.abs(key_col - (col - low_col)) <= reach_col.astype(jnp.float32)
            )
            for row in range(classes):
                row_ok = jnp.abs(key_row - row) <= reach_row.astype(jnp.float32)
                shift = jnp.where(col_ok & row_ok, 0.0, MASKED)
                low = (col - start) * strip + row * half
                masked = scores[low : low + half, :] + shift
                top = jnp.max(masked, axis=1, keepdims=True)
                weights.append(jnp.exp2((masked - top) * scale))
        weights = jnp.concatenate(weights, 0).astype(jnp.bfloat16)
        sums = jnp.dot(weights, vs_ref[key_rows, :], preferred_element_type=jnp.float32)
        result = sums[:, :HEAD_DIM] / sums[:, HEAD_DIM:]
        for col in range(start, start + block_cols):
            for row in range(rows):
                low = row * FRAME_W + col * TILE_W
                got = (col - start) * strip + row * TILE_W
                lin_out_ref[low : low + TILE_W, :] = result[got : got + TILE_W, :]
    tokens = slots * chunk
    lin_out_ref[tokens:, :] = jnp.zeros(
        (lin_out_ref.shape[0] - tokens, HEAD_DIM), jnp.float32
    )
    for slot in range(slots):
        low = slot * chunk
        out_ref[slot] = lin_out_ref[low : low + slot_rows, :].astype(jnp.bfloat16)


def attend(meta, q, kv, before, after, chunk):
    slots, slot_rows, width = q.shape
    heads = width // HEAD_DIM
    tokens = slots * chunk
    lin_rows = padded(tokens + slot_rows - chunk)
    block = (slots, slot_rows, HEAD_DIM)
    own = pl.BlockSpec(block, lambda h: (0, 0, h))
    second = pl.BlockSpec(block, lambda h: (0, 0, h + heads))
    return pl.pallas_call(
        functools.partial(attend_kernel, chunk=chunk, block_cols=2, reach=2),
        out_shape=jax.ShapeDtypeStruct(q.shape, jnp.bfloat16),
        grid=(heads,),
        in_specs=[pl.BlockSpec(memory_space=pltpu.SMEM), own] + [own] * 3 + [second] * 3,
        out_specs=own,
        scratch_shapes=[
            pltpu.VMEM((lin_rows, HEAD_DIM), jnp.float32),
            pltpu.VMEM((tokens, HEAD_DIM), jnp.bfloat16),
            pltpu.VMEM((3 * tokens, HEAD_DIM), jnp.bfloat16),
            pltpu.VMEM((3 * tokens, 2 * HEAD_DIM), jnp.bfloat16),
            pltpu.VMEM((lin_rows, HEAD_DIM), jnp.float32),
        ],
        compiler_params=pltpu.CompilerParams(vmem_limit_bytes=32 * 2**20),
    )(meta, q, before, kv, after, before, kv, after)


def neighbours(slabs, groups, step):
    turned = [groups // 2 if slab >= slabs // 2 else 0 for slab in range(slabs)]
    pairs = []
    for slab in range(slabs):
        other = slab + step
        if 0 <= other < slabs:
            for group in range(groups):
                pairs.append(
                    (
                        slab * groups + (group ^ turned[slab]),
                        other * groups + (group ^ turned[other]),
                    )
                )
    return pairs


def swap(slots):
    return lax.all_to_all(slots, "head", split_axis=0, concat_axis=0)


def per_device(q_vals, k_vals, v_vals, q_scale, k_scale, v_scale, window):
    groups = lax.axis_size("head")
    slabs = lax.axis_size("slab")
    chunk = q_vals.shape[0]
    local_heads = q_scale.shape[1] // groups
    slab = lax.axis_index("slab")
    flip = jnp.where(slab >= slabs // 2, groups // 2, 0).astype(jnp.int32)
    group = lax.axis_index("head") ^ flip
    reach = lax.dynamic_slice_in_dim(window, group * local_heads, local_heads, 0)
    ends = jnp.stack([jnp.where(slab > 0, 0, 1), jnp.where(slab < slabs - 1, 2, 1)])
    meta = jnp.concatenate([reach.reshape(-1), ends.astype(jnp.int32)])
    flip = flip.reshape(1)
    both = ("slab", "head")
    kv = swap(pack(flip, [(k_vals, k_scale), (v_vals, v_scale)], groups))
    before = lax.ppermute(kv, both, neighbours(slabs, groups, 1))
    after = lax.ppermute(kv, both, neighbours(slabs, groups, -1))
    q = swap(pack(flip, [(q_vals, q_scale)], groups))
    attended = attend(meta, q, kv, before, after, chunk)
    return unpack(flip, swap(attended), chunk)


def solution(mesh):
    tokens = P(("slab", "head"), None)
    return jax.shard_map(
        per_device,
        mesh=mesh,
        in_specs=(tokens,) * 6 + (P(),),
        out_specs=tokens,
        check_vma=False,
    )
```

time: 150 us -> 80.3 us (0.54)
  the two profiles are of different devices: /device:TPU:1 before, /device:TPU:16 now
where the time goes in v1:
time: 80.3 us; the launch traced here: 79.8 us
  blocking collectives  37.1 us (46%)
  starting transfers between devices  14.5 us (18%)
  waiting for transfers between devices  13.6 us (17%)
  Pallas kernels  9.48 us (12%)
  local copies, waits for them, and re-layouts  5.01 us (6%)
    all_to_all x2, blocking collectives, swap(): return lax.all_to_all(slots, 'head', split_axis=0, concat_axis=0)  37.1 us
    all_to_all x1, waiting for transfers between devices, swap(): return lax.all_to_all(slots, 'head', split_axis=0, concat_axis=0)  8.96 us
    ppermute x1, starting transfers between devices, per_device(): after = lax.ppermute(kv, both, neighbours(slabs, groups, -1))  8.89 us
    pallas_call x1, Pallas kernels, attend(): pl.pallas_call(functools.partial(attend_kernel, chunk=chunk, block_cols=2...  7.77 us
    unnamed x15, local copies, waits for them, and re-layouts  4.76 us
    ppermute x1, waiting for transfers between devices, per_device(): before = lax.ppermute(kv, both, neighbours(slabs, groups, 1))  4.61 us
    all_to_all x1, starting transfers between devices, swap(): return lax.all_to_all(slots, 'head', split_axis=0, concat_axis=0)  3.68 us
    ppermute x1, starting transfers between devices, per_device(): before = lax.ppermute(kv, both, neighbours(slabs, groups, 1))  1.92 us
  transfers between devices with their start and end apart: 3, of which 2 were waited for; matrix products, arithmetic and copies ran while one was open for 1% of the time, Pallas kernels for 0%

profile of v1, /device:TPU:16, one launch (start us, length us, event | category | flops | bytes accessed | tf_op | source)
XLA Modules:
  0.0 79.8 jit_solution(1374504845054376310)
XLA Ops:
  0.0 0.0 copy-start
  0.0 0.8 %copy.10.refs_1_ = bf16[100,24]{1,0:T(8,128)(2,1)S(1)} copy(bf16[100,24]{0,1:T(8,128)(2,1)} %param.11) | data formatting | bytes 9600 | tf_op args[4]
  0.8 0.8 %copy.11.refs_3_ = bf16[100,24]{1,0:T(8,128)(2,1)S(1)} copy(bf16[100,24]{0,1:T(8,128)(2,1)} %param.12) | data formatting | bytes 9600 | tf_op args[5]
  1.6 0.0 copy-start.3
  1.6 1.1 %copy-done.3 = bf16[100,3072]{1,0:T(8,128)(2,1)S(1)} copy-done((bf16[100,3072]{1,0:T(8,128)(2,1)S(1)}, bf16[100,3072]{1,0:T(8,128)(2,1)}, u32[]{:S(2)}) %copy-start.3) | copy-done | bytes 614424
  2.7 0.0 copy-start.4
  2.7 1.1 %copy-done.4 = bf16[100,3072]{1,0:T(8,128)(2,1)S(1)} copy-done((bf16[100,3072]{1,0:T(8,128)(2,1)S(1)}, bf16[100,3072]{1,0:T(8,128)(2,1)}, u32[]{:S(2)}) %copy-start.4) | copy-done | bytes 614424
  3.8 0.5 shard_map.74
  4.3 0.0 copy-start.5
  4.4 0.0 copy-start.2
  4.4 23.1 %all_to_all.15.refs_1_.refs_4_ = bf16[8,104,768]{2,1,0:T(8,128)(2,1)S(1)} all-to-all(bf16[8,104,768]{2,1,0:T(8,128)(2,1)S(1)} %shard_map.74), channel_id=1, replica_groups=mesh['slab'=64,'head'=8] {'head'}, dimensions={0} | all-to-all | bytes 2555904 | tf_op jit(solution)/shard_map/all_to_all | solution.py:226
  27.5 8.9 %collective-permute-start.1 = (bf16[8,104,768]{2,1,0:T(8,128)(2,1)S(1)}, bf16[8,104,768]{2,1,0:T(8,128)(2,1)S(1)}, u32[]{:S(2)}, u32[]{:S(2)}) collective-permute-start(bf16[8,104,768]{2,1,0:T(8,128)(2,1)S(1)} %all_to_all.15.refs_1_.refs_4_), channel_id=1, source_target_pairs={{8,0},{9,1},{10,2},{11,3},{12,4},{13,5},{14,6},{15,7},{16,8},{17,9... | collective-permute-start | bytes 3833864 | tf_op jit(solution)/shard_map/ppermute | solution.py:244
  36.4 1.9 %collective-permute-start = (bf16[8,104,768]{2,1,0:T(8,128)(2,1)S(1)}, bf16[8,104,768]{2,1,0:T(8,128)(2,1)}, u32[]{:S(2)}, u32[]{:S(2)}) collective-permute-start(bf16[8,104,768]{2,1,0:T(8,128)(2,1)S(1)} %all_to_all.15.refs_1_.refs_4_), channel_id=1, source_target_pairs={{0,8},{1,9},{2,10},{3,11},{4,12},{5,13},{6,14},{7,15},{8,16},{9,17... | collective-permute-start | bytes 3833864 | tf_op jit(solution)/shard_map/ppermute | solution.py:243
  38.3 0.0 copy-done.5
  38.3 0.1 copy.9.refs_1_
  38.4 0.0 copy-done.2
  38.4 0.3 shard_map.73
  38.7 0.0 copy-start.1
  38.7 0.8 %copy-done.1 = bf16[8,104,384]{2,1,0:T(8,128)(2,1)} copy-done((bf16[8,104,384]{2,1,0:T(8,128)(2,1)}, bf16[8,104,384]{2,1,0:T(8,128)(2,1)S(1)}, u32[]{:S(2)}) %copy-start.1) | copy-done | bytes 639000
  39.6 3.7 %all-to-all-start = ((bf16[8,104,384]{2,1,0:T(8,128)(2,1)}), bf16[8,104,384]{2,1,0:T(8,128)(2,1)S(1)}, u32[]{:S(2)}, u32[]{:S(2)}) async-start(bf16[8,104,384]{2,1,0:T(8,128)(2,1)} %copy-done.1), calls=%async_computation | async-start | bytes 1277952 | tf_op jit(solution)/shard_map/all_to_all | solution.py:226
  43.3 0.0 copy-done
  43.3 0.1 constant_dynamic-slice_fusion
  43.3 0.1 copy.8
  43.4 0.1 reshape.7
  43.5 0.1 pad_add_fusion.meta_ref
  43.6 9.0 %all-to-all-done.q_ref = bf16[8,104,384]{2,1,0:T(8,128)(2,1)S(1)} async-done(((bf16[8,104,384]{2,1,0:T(8,128)(2,1)}), bf16[8,104,384]{2,1,0:T(8,128)(2,1)S(1)}, u32[]{:S(2)}, u32[]{:S(2)}) %all-to-all-start) | async-done | bytes 639008 | tf_op jit(solution)/shard_map/all_to_all | solution.py:226
  52.6 0.0 collective-permute-done.1.refs_2_.refs_5_
  52.6 4.6 %collective-permute-done.refs_0_.refs_3_ = bf16[8,104,768]{2,1,0:T(8,128)(2,1)} collective-permute-done((bf16[8,104,768]{2,1,0:T(8,128)(2,1)S(1)}, bf16[8,104,768]{2,1,0:T(8,128)(2,1)}, u32[]{:S(2)}, u32[]{:S(2)}) %collective-permute-start) | collective-permute-done | bytes 1277984 | tf_op jit(solution)/shard_map/ppermute | solution.py:243
  57.2 7.8 %shard_map.75 = bf16[8,104,384]{2,1,0:T(8,128)(2,1)S(1)} custom-call(s32[11]{0:T(128)S(1)} %pad_add_fusion.meta_ref, bf16[8,104,384]{2,1,0:T(8,128)(2,1)S(1)} %all-to-all-done.q_ref, bf16[8,104,768]{2,1,0:T(8,128)(2,1)} %collective-permute-done.refs_0_.refs_3_, bf16[8,104,768]{2,1,0:T(8,128)(2,1)S(1)} %all_to_all.15.refs_1_.refs_4_, ...), custom_call_target="tpu_custom_call" | custom-call | tf_op jit(solution)/shard_map/pallas_call | solution.py:192
  64.9 14.0 %all_to_all.16.in_ref = bf16[8,104,384]{2,1,0:T(8,128)(2,1)S(1)} all-to-all(bf16[8,104,384]{2,1,0:T(8,128)(2,1)S(1)} %shard_map.75), channel_id=1, replica_groups=mesh['slab'=64,'head'=8] {'head'}, dimensions={0} | all-to-all | bytes 1277952 | tf_op jit(solution)/shard_map/all_to_all | solution.py:226
  78.9 0.9 %shard_map.76 = bf16[100,3072]{1,0:T(8,128)(2,1)} custom-call(s32[1]{0:T(128)} %bitcast.flip_ref, bf16[8,104,384]{2,1,0:T(8,128)(2,1)S(1)} %all_to_all.16.in_ref), custom_call_target="tpu_custom_call" | custom-call | tf_op jit(solution)/shard_map/pallas_call | solution.py:80
Async XLA Ops:
  0.0 43.3 %copy-start = (s32[24,3]{0,1:T(4,128)S(1)}, s32[24,3]{0,1:T(4,128)}, u32[]{:S(2)}) copy-start(s32[24,3]{0,1:T(4,128)} %param.13) | copy-start | bytes 868
  1.6 1.1 %copy-start.3 = (bf16[100,3072]{1,0:T(8,128)(2,1)S(1)}, bf16[100,3072]{1,0:T(8,128)(2,1)}, u32[]{:S(2)}) copy-start(bf16[100,3072]{1,0:T(8,128)(2,1)} %refs_0_.3) | copy-start | bytes 1843204
  2.7 1.1 %copy-start.4 = (bf16[100,3072]{1,0:T(8,128)(2,1)S(1)}, bf16[100,3072]{1,0:T(8,128)(2,1)}, u32[]{:S(2)}) copy-start(bf16[100,3072]{1,0:T(8,128)(2,1)} %refs_2_.1) | copy-start | bytes 1843204
  4.3 34.0 %copy-start.5 = (bf16[100,24]{0,1:T(8,128)(2,1)S(1)}, bf16[100,24]{0,1:T(8,128)(2,1)}, u32[]{:S(2)}) copy-start(bf16[100,24]{0,1:T(8,128)(2,1)} %param.10) | copy-start | bytes 14404
  4.4 34.1 %copy-start.2 = (bf16[100,3072]{1,0:T(8,128)(2,1)S(1)}, bf16[100,3072]{1,0:T(8,128)(2,1)}, u32[]{:S(2)}) copy-start(bf16[100,3072]{1,0:T(8,128)(2,1)} %refs_0_.2) | copy-start | bytes 1843204
  27.5 25.1 %collective-permute-start.1 = (bf16[8,104,768]{2,1,0:T(8,128)(2,1)S(1)}, bf16[8,104,768]{2,1,0:T(8,128)(2,1)S(1)}, u32[]{:S(2)}, u32[]{:S(2)}) collective-permute-start(bf16[8,104,768]{2,1,0:T(8,128)(2,1)S(1)} %all_to_all.15.refs_1_.refs_4_), channel_id=1, source_target_pairs={{8,0},{9,1},{10,2},{11,3},{12,4},{13,5},{14,6},{15,7},{16,8},{17,9... | collective-permute-start | bytes 3833864 | tf_op jit(solution)/shard_map/ppermute | solution.py:244
  36.4 20.8 %collective-permute-start = (bf16[8,104,768]{2,1,0:T(8,128)(2,1)S(1)}, bf16[8,104,768]{2,1,0:T(8,128)(2,1)}, u32[]{:S(2)}, u32[]{:S(2)}) collective-permute-start(bf16[8,104,768]{2,1,0:T(8,128)(2,1)S(1)} %all_to_all.15.refs_1_.refs_4_), channel_id=1, source_target_pairs={{0,8},{1,9},{2,10},{3,11},{4,12},{5,13},{6,14},{7,15},{8,16},{9,17... | collective-permute-start | bytes 3833864 | tf_op jit(solution)/shard_map/ppermute | solution.py:243
  38.7 0.8 %copy-start.1 = (bf16[8,104,384]{2,1,0:T(8,128)(2,1)}, bf16[8,104,384]{2,1,0:T(8,128)(2,1)S(1)}, u32[]{:S(2)}) copy-start(bf16[8,104,384]{2,1,0:T(8,128)(2,1)S(1)} %shard_map.73) | copy-start | bytes 1916932
  39.6 13.0 %all-to-all-start = ((bf16[8,104,384]{2,1,0:T(8,128)(2,1)}), bf16[8,104,384]{2,1,0:T(8,128)(2,1)S(1)}, u32[]{:S(2)}, u32[]{:S(2)}) async-start(bf16[8,104,384]{2,1,0:T(8,128)(2,1)} %copy-done.1), calls=%async_computation | async-start | bytes 1277952 | tf_op jit(solution)/shard_map/all_to_all | solution.py:226

commit v2 on v1

v2 whole, which is shorter than its diff:
```python
import functools

import jax
import jax.numpy as jnp
from jax import lax
from jax.experimental import pallas as pl
from jax.experimental.pallas import tpu as pltpu
from jax.sharding import PartitionSpec as P

TILE_H = 5
TILE_W = 8
FRAME_W = 80
HEAD_DIM = 128
MASKED = -1e30
BLOCK_COLS = 2
MOST_COLS = 2
SCALE = 1.4426950408889634 / HEAD_DIM**0.5
VMEM_LIMIT = 32 * 2**20


def geometry(tokens):
    rows = tokens // FRAME_W
    return rows, FRAME_W // TILE_W, rows * TILE_W


def padded(rows):
    return -(-rows // 8) * 8


def params():
    return pltpu.CompilerParams(vmem_limit_bytes=VMEM_LIMIT)


def in_smem():
    return pl.BlockSpec(memory_space=pltpu.SMEM)


def in_vmem():
    return pl.BlockSpec(memory_space=pltpu.VMEM)


def pack_kernel(
    flip_ref, k_ref, v_ref, q_ref, ks_ref, vs_ref, qs_ref, kv_out, q_out, buf, scale_buf, sems
):
    groups, slot_rows, width = q_out.shape
    rows = k_ref.shape[0]
    heads = width // HEAD_DIM
    places = ((kv_out, 0), (kv_out, width), (q_out, 0))
    copies = [
        pltpu.make_async_copy(source, scale_buf.at[at], sems.at[at])
        for at, source in enumerate((ks_ref, vs_ref, qs_ref))
    ] + [
        pltpu.make_async_copy(source, buf.at[at], sems.at[len(places) + at])
        for at, source in enumerate((k_ref, v_ref, q_ref))
    ]
    for copy in copies:
        copy.start()
    for copy in copies:
        copy.wait()
    blank = jnp.zeros((slot_rows - rows, HEAD_DIM), jnp.float32)
    for at, (out_ref, low) in enumerate(places):
        scales = scale_buf[at].astype(jnp.float32).T
        for group in range(groups):
            for head in range(heads):
                index = group * heads + head
                vals = buf[at, :, index * HEAD_DIM : (index + 1) * HEAD_DIM]
                wide = vals.astype(jnp.float32) * scales[:, index : index + 1]
                if slot_rows > rows:
                    wide = jnp.concatenate([wide, blank], 0)
                start = low + head * HEAD_DIM
                out_ref[group ^ flip_ref[0], :, start : start + HEAD_DIM] = wide.astype(
                    jnp.bfloat16
                )


def pack(flip, k_vals, v_vals, q_vals, k_scale, v_scale, q_scale):
    groups = lax.axis_size("head")
    rows, full = k_vals.shape
    width = full // groups
    slot_rows = padded(rows)
    operands = [
        pltpu.with_memory_space_constraint(x, pltpu.HBM)
        for x in (k_vals, v_vals, q_vals, k_scale.T, v_scale.T, q_scale.T)
    ]
    return pl.pallas_call(
        pack_kernel,
        out_shape=(
            jax.ShapeDtypeStruct((groups, slot_rows, 2 * width), jnp.bfloat16),
            jax.ShapeDtypeStruct((groups, slot_rows, width), jnp.bfloat16),
        ),
        in_specs=[in_smem()] + [pl.BlockSpec(memory_space=pltpu.HBM)] * 6,
        out_specs=(in_vmem(), in_vmem()),
        scratch_shapes=[
            pltpu.VMEM((3, rows, full), jnp.bfloat16),
            pltpu.VMEM((3, k_scale.shape[1], rows), jnp.bfloat16),
            pltpu.SemaphoreType.DMA((6,)),
        ],
        compiler_params=params(),
    )(flip, *operands)


def unpack_kernel(flip_ref, in_ref, out_ref):
    groups, _, width = in_ref.shape
    rows = out_ref.shape[0]
    for group in range(groups):
        slot = in_ref[group ^ flip_ref[0]]
        out_ref[:, group * width : (group + 1) * width] = slot[:rows]


def unpack(flip, slots, rows):
    groups, _, width = slots.shape
    return pl.pallas_call(
        unpack_kernel,
        out_shape=jax.ShapeDtypeStruct((rows, groups * width), jnp.bfloat16),
        in_specs=[in_smem(), in_vmem()],
        out_specs=in_vmem(),
        compiler_params=params(),
    )(flip, slots)


def by_columns(slots_ref, lanes, lin_ref, chunk):
    slots = slots_ref.shape[0]
    rows, cols, _ = geometry(slots * chunk)
    for slot in range(slots):
        part = slots_ref[slot, :, lanes].astype(jnp.float32)
        lin_ref[slot * chunk : slot * chunk + part.shape[0], :] = part
    for col in range(cols):
        pieces = []
        for row in range(rows):
            low = row * FRAME_W + col * TILE_W
            pieces.append(lin_ref[low : low + TILE_W, :])
        yield col, jnp.concatenate(pieces, 0)


def blocks(cols, strip, span):
    found = []
    for start in range(0, cols, BLOCK_COLS):
        low = max(0, start - MOST_COLS)
        high = min(cols, start + BLOCK_COLS + MOST_COLS)
        query = slice(start * strip, (start + BLOCK_COLS) * strip)
        key = slice(low * span * strip, high * span * strip)
        found.append((start, low, query, key))
    return found


def shifts(block, strip, rows, frames, frame_reach, row_reach, col_reach):
    start, low_col, _, key = block
    span = len(frames)
    half = strip * TILE_H // rows
    at = lax.broadcasted_iota(jnp.int32, (1, key.stop - key.start), 1).astype(jnp.float32)
    key_col = jnp.floor((at + 0.5) * (1.0 / (span * strip)))
    rest = at - key_col * (span * strip)
    key_frame = jnp.floor((rest + 0.5) * (1.0 / strip))
    rest = rest - key_frame * strip
    key_row = jnp.floor((rest + 0.5) * (1.0 / half))
    gap = jnp.zeros_like(at)
    for frame, far in enumerate(frames):
        gap = jnp.where(key_frame == frame, far, gap)
    frame_ok = gap <= frame_reach
    for col in range(start, start + BLOCK_COLS):
        col_ok = frame_ok & (jnp.abs(key_col - (col - low_col)) <= col_reach)
        for row in range(rows // TILE_H):
            row_ok = jnp.abs(key_row - row) <= row_reach
            low = (col - start) * strip + row * half
            yield slice(low, low + half), jnp.where(col_ok & row_ok, 0.0, MASKED)


def attend_kernel(
    meta_ref, q_ref, own_ref, beside_ref, away_ref, out_ref, lin_ref, qs_ref, ks_ref, vs_ref,
    lin_out_ref, *, chunk,
):
    slots, slot_rows, width = out_ref.shape
    heads = width // HEAD_DIM
    tokens = slots * chunk
    rows, cols, strip = geometry(tokens)
    sources = (own_ref, beside_ref, away_ref)
    span = len(sources)
    vs_ref[:, HEAD_DIM:] = jnp.ones((vs_ref.shape[0], vs_ref.shape[1] - HEAD_DIM), vs_ref.dtype)
    lin_out_ref[tokens:, :] = jnp.zeros((lin_out_ref.shape[0] - tokens, HEAD_DIM), jnp.float32)
    away = jnp.where(meta_ref[3 * heads] > 0, 1.0, 2.0)

    @pl.loop(0, heads)
    def _(head):
        lanes = pl.ds(pl.multiple_of(head * HEAD_DIM, HEAD_DIM), HEAD_DIM)
        value_lanes = pl.ds(pl.multiple_of((heads + head) * HEAD_DIM, HEAD_DIM), HEAD_DIM)
        for col, part in by_columns(q_ref, lanes, lin_ref, chunk):
            qs_ref[col * strip : (col + 1) * strip, :] = part.astype(jnp.bfloat16)
        for frame, source in enumerate(sources):
            for take, target in ((lanes, ks_ref), (value_lanes, vs_ref)):
                for col, part in by_columns(source, take, lin_ref, chunk):
                    low = (col * span + frame) * strip
                    target[low : low + strip, :HEAD_DIM] = part.astype(jnp.bfloat16)
        reach = [meta_ref[3 * head + i].astype(jnp.float32) for i in range(3)]
        all_blocks = blocks(cols, strip, span)
        all_scores = [
            lax.dot_general(
                qs_ref[query, :],
                ks_ref[key, :],
                (((1,), (1,)), ((), ())),
                preferred_element_type=jnp.float32,
            )
            for _, _, query, key in all_blocks
        ]
        all_weights = []
        for block, scores in zip(all_blocks, all_scores):
            weights = []
            for mine, shift in shifts(block, strip, rows, (0.0, 1.0, away), *reach):
                masked = scores[mine, :] + shift
                top = jnp.max(masked, axis=1, keepdims=True)
                weights.append(jnp.exp2((masked - top) * SCALE))
            all_weights.append(jnp.concatenate(weights, 0).astype(jnp.bfloat16))
        for (start, _, _, key), weights in zip(all_blocks, all_weights):
            sums = jnp.dot(weights, vs_ref[key, :], preferred_element_type=jnp.float32)
            result = sums[:, :HEAD_DIM] / sums[:, HEAD_DIM:]
            for col in range(start, start + BLOCK_COLS):
                for row in range(rows):
                    low = row * FRAME_W + col * TILE_W
                    got = (col - start) * strip + row * TILE_W
                    lin_out_ref[low : low + TILE_W, :] = result[got : got + TILE_W, :]
        for slot in range(slots):
            low = slot * chunk
            out_ref[slot, :, lanes] = lin_out_ref[low : low + slot_rows, :].astype(jnp.bfloat16)


def attend(meta, q, own, beside, away, chunk):
    slots, slot_rows, width = q.shape
    tokens = slots * chunk
    lin_rows = padded(tokens + slot_rows - chunk)
    return pl.pallas_call(
        functools.partial(attend_kernel, chunk=chunk),
        out_shape=jax.ShapeDtypeStruct(q.shape, jnp.bfloat16),
        in_specs=[in_smem()] + [in_vmem()] * 4,
        out_specs=in_vmem(),
        scratch_shapes=[
            pltpu.VMEM((lin_rows, HEAD_DIM), jnp.float32),
            pltpu.VMEM((tokens, HEAD_DIM), jnp.bfloat16),
            pltpu.VMEM((3 * tokens, HEAD_DIM), jnp.bfloat16),
            pltpu.VMEM((3 * tokens, 2 * HEAD_DIM), jnp.bfloat16),
            pltpu.VMEM((lin_rows, HEAD_DIM), jnp.float32),
        ],
        compiler_params=params(),
    )(meta, q, own, beside, away)


def turn(slab, slabs, groups):
    return jnp.where(slab >= slabs // 2, groups // 2, 0)


def exchange(array, pairs):
    groups, slabs = lax.axis_size("head"), lax.axis_size("slab")
    turned = [0 if slab < slabs // 2 else groups // 2 for slab in range(slabs)]
    both = [
        (a * groups + (group ^ turned[a]), b * groups + (group ^ turned[b]))
        for low, high in pairs
        for a, b in ((low, high), (high, low))
        for group in range(groups)
    ]
    return lax.ppermute(array, ("slab", "head"), both)


def swap(slots):
    return lax.all_to_all(slots, "head", split_axis=0, concat_axis=0)


def per_device(q_vals, k_vals, v_vals, q_scale, k_scale, v_scale, window):
    groups = lax.axis_size("head")
    slabs = lax.axis_size("slab")
    chunk = q_vals.shape[0]
    local_heads = q_scale.shape[1] // groups
    slab = lax.axis_index("slab")
    flip = turn(slab, slabs, groups).astype(jnp.int32)
    low = (lax.axis_index("head") ^ flip) * local_heads
    flip = flip.reshape(1)
    reach = lax.dynamic_slice_in_dim(window, low, local_heads, 0)
    linked = ((slab > 0) & (slab < slabs - 1)).astype(jnp.int32)
    meta = jnp.concatenate([reach.reshape(-1), linked.reshape(1)])
    kv, q = pack(flip, k_vals, v_vals, q_vals, k_scale, v_scale, q_scale)
    kv = swap(kv)
    beside = exchange(kv, [(s, s + 1) for s in range(0, slabs, 2)])
    away = exchange(kv, [(s, s + 1) for s in range(1, slabs - 1, 2)])
    q = swap(q)
    attended = attend(meta, q, kv, beside, away, chunk)
    return unpack(flip, swap(attended), chunk)


def solution(mesh):
    tokens = P(("slab", "head"), None)
    return jax.shard_map(
        per_device,
        mesh=mesh,
        in_specs=(tokens,) * 6 + (P(),),
        out_specs=tokens,
        check_vma=False,
    )
```

time: 80.3 us -> 74.3 us (0.925)
  local copies, waits for them, and re-layouts: 5.01 us -> 0.27 us
  waiting for transfers between devices: 13.6 us -> 11.7 us
  Pallas kernels: 9.48 us -> 10.4 us
    unnamed x15 -> x4, local copies, waits for them, and re-layouts: 4.76 us -> 0.01 us
    ppermute x2, waiting for transfers between devices: 4.61 us -> 0.01 us  [exchange(): return lax.ppermute(array, ('slab', 'head'), both)]
    all_to_all x1, waiting for transfers between devices: 8.96 us -> 11.7 us  [swap(): return lax.all_to_all(slots, 'head', split_axis=0, concat_axis=0)]
    pallas_call x3 -> x2, Pallas kernels: 8.59 us -> 9.51 us  [the longest x1 7.01 us: attend(): pl.pallas_call(functools.partial(attend_kernel, chunk=chunk), out_shape=j...]
  transfers between devices with their start and end apart: 3 -> 3, of which waited for: 2 -> 1; matrix products, arithmetic and copies ran while one was open for 1% -> 0% of each run, Pallas kernels for 0% -> 0%
where the time goes in v2:
time: 74.3 us; the launch traced here: 73.9 us
  blocking collectives  36.9 us (50%)
  starting transfers between devices  14.5 us (20%)
  waiting for transfers between devices  11.7 us (16%)
  Pallas kernels  10.4 us (14%)
    all_to_all x2, blocking collectives, swap(): return lax.all_to_all(slots, 'head', split_axis=0, concat_axis=0)  36.9 us
    all_to_all x1, waiting for transfers between devices, swap(): return lax.all_to_all(slots, 'head', split_axis=0, concat_axis=0)  11.7 us
    ppermute x2, starting transfers between devices, exchange(): return lax.ppermute(array, ('slab', 'head'), both)  10.8 us
    pallas_call x1, Pallas kernels, attend(): pl.pallas_call(functools.partial(attend_kernel, chunk=chunk), out_shape=j...  7.01 us
    all_to_all x1, starting transfers between devices, swap(): return lax.all_to_all(slots, 'head', split_axis=0, concat_axis=0)  3.7 us
    pallas_call x1, Pallas kernels, pack(): pl.pallas_call(pack_kernel, out_shape=(jax.ShapeDtypeStruct((groups, slot...  2.5 us
  transfers between devices with their start and end apart: 3, of which 1 were waited for; matrix products, arithmetic and copies ran while one was open for 0% of the time, Pallas kernels for 0%

profile of v2, /device:TPU:16, one launch (start us, length us, event | category | flops | bytes accessed | tf_op | source)
XLA Modules:
  0.0 73.9 jit_solution(17227413361110615363)
XLA Ops:
  0.0 0.0 copy-start
  0.0 2.5 %shard_map.73 = (bf16[8,104,768]{2,1,0:T(8,128)(2,1)S(1)}, bf16[8,104,384]{2,1,0:T(8,128)(2,1)S(1)}) custom-call(s32[1]{0:T(128)} %bitcast.flip_ref, bf16[100,3072]{1,0:T(8,128)(2,1)} %k_ref.1, bf16[100,3072]{1,0:T(8,128)(2,1)} %v_ref.1, bf16[100,3072]{1,0:T(8,128)(2,1)} %q_ref.1, bf16[24,100]{1,0:T(8,128)(2,1)} %bitcast.5, bf16[24,100]{1,0:T(8,128)(2,1)} %bitcast.6, ...), custom_call_target="tpu_custom_call" | custom-call | tf_op jit(solution)/shard_map/pallas_call | solution.py:85
  2.5 0.0 copy-start.1
  2.5 23.0 %all_to_all.15.own_ref = bf16[8,104,768]{2,1,0:T(8,128)(2,1)S(1)} all-to-all(bf16[8,104,768]{2,1,0:T(8,128)(2,1)S(1)} %get-tuple-element.8), channel_id=1, replica_groups=mesh['slab'=64,'head'=8] {'head'}, dimensions={0} | all-to-all | bytes 2555904 | tf_op jit(solution)/shard_map/all_to_all | solution.py:262
  25.5 0.0 copy-done.1
  25.5 8.9 %collective-permute-start.1 = (bf16[8,104,768]{2,1,0:T(8,128)(2,1)S(1)}, bf16[8,104,768]{2,1,0:T(8,128)(2,1)S(1)}, u32[]{:S(2)}, u32[]{:S(2)}) collective-permute-start(bf16[8,104,768]{2,1,0:T(8,128)(2,1)S(1)} %all_to_all.15.own_ref), channel_id=1, source_target_pairs={{8,16},{9,17},{10,18},{11,19},{12,20},{13,21},{14,22},{15,23},{16,... | collective-permute-start | bytes 3833864 | tf_op jit(solution)/shard_map/ppermute | solution.py:258
  34.4 1.9 %collective-permute-start = (bf16[8,104,768]{2,1,0:T(8,128)(2,1)S(1)}, bf16[8,104,768]{2,1,0:T(8,128)(2,1)}, u32[]{:S(2)}, u32[]{:S(2)}) collective-permute-start(bf16[8,104,768]{2,1,0:T(8,128)(2,1)S(1)} %all_to_all.15.own_ref), channel_id=1, source_target_pairs={{0,8},{1,9},{2,10},{3,11},{4,12},{5,13},{6,14},{7,15},{8,0},{9,1},... | collective-permute-start | bytes 3833864 | tf_op jit(solution)/shard_map/ppermute | solution.py:258
  36.3 3.7 %all-to-all-start = ((bf16[8,104,384]{2,1,0:T(8,128)(2,1)}), bf16[8,104,384]{2,1,0:T(8,128)(2,1)S(1)}, u32[]{:S(2)}, u32[]{:S(2)}) async-start(bf16[8,104,384]{2,1,0:T(8,128)(2,1)} %copy-done.1), calls=%async_computation | async-start | bytes 1277952 | tf_op jit(solution)/shard_map/all_to_all | solution.py:262
  40.0 0.0 copy-done
  40.0 0.1 constant_dynamic-slice_fusion
  40.1 0.1 copy.8
  40.2 0.1 reshape.13
  40.3 0.1 pad_add_fusion.meta_ref
  40.4 11.7 %all-to-all-done.q_ref = bf16[8,104,384]{2,1,0:T(8,128)(2,1)S(1)} async-done(((bf16[8,104,384]{2,1,0:T(8,128)(2,1)}), bf16[8,104,384]{2,1,0:T(8,128)(2,1)S(1)}, u32[]{:S(2)}, u32[]{:S(2)}) %all-to-all-start) | async-done | bytes 639008 | tf_op jit(solution)/shard_map/all_to_all | solution.py:262
  52.1 0.0 collective-permute-done.1.away_ref
  52.1 0.0 collective-permute-done.beside_ref
  52.1 7.0 %shard_map.74 = bf16[8,104,384]{2,1,0:T(8,128)(2,1)S(1)} custom-call(s32[10]{0:T(128)S(1)} %pad_add_fusion.meta_ref, bf16[8,104,384]{2,1,0:T(8,128)(2,1)S(1)} %all-to-all-done.q_ref, bf16[8,104,768]{2,1,0:T(8,128)(2,1)S(1)} %all_to_all.15.own_ref, bf16[8,104,768]{2,1,0:T(8,128)(2,1)} %collective-permute-done.beside_ref, ...), custom_call_target="tpu_custom_call" | custom-call | tf_op jit(solution)/shard_map/pallas_call | solution.py:229
  59.1 13.9 %all_to_all.16.in_ref = bf16[8,104,384]{2,1,0:T(8,128)(2,1)S(1)} all-to-all(bf16[8,104,384]{2,1,0:T(8,128)(2,1)S(1)} %shard_map.74), channel_id=1, replica_groups=mesh['slab'=64,'head'=8] {'head'}, dimensions={0} | all-to-all | bytes 1277952 | tf_op jit(solution)/shard_map/all_to_all | solution.py:262
  73.0 0.9 %shard_map.75 = bf16[100,3072]{1,0:T(8,128)(2,1)} custom-call(s32[1]{0:T(128)} %bitcast.flip_ref, bf16[8,104,384]{2,1,0:T(8,128)(2,1)S(1)} %all_to_all.16.in_ref), custom_call_target="tpu_custom_call" | custom-call | tf_op jit(solution)/shard_map/pallas_call | solution.py:112
Async XLA Ops:
  0.0 40.0 %copy-start = (s32[24,3]{0,1:T(4,128)S(1)}, s32[24,3]{0,1:T(4,128)}, u32[]{:S(2)}) copy-start(s32[24,3]{0,1:T(4,128)} %param.13) | copy-start | bytes 868
  2.5 23.0 %copy-start.1 = (bf16[8,104,384]{2,1,0:T(8,128)(2,1)}, bf16[8,104,384]{2,1,0:T(8,128)(2,1)S(1)}, u32[]{:S(2)}) copy-start(bf16[8,104,384]{2,1,0:T(8,128)(2,1)S(1)} %get-tuple-element.7) | copy-start | bytes 1916932
  25.5 26.6 %collective-permute-start.1 = (bf16[8,104,768]{2,1,0:T(8,128)(2,1)S(1)}, bf16[8,104,768]{2,1,0:T(8,128)(2,1)S(1)}, u32[]{:S(2)}, u32[]{:S(2)}) collective-permute-start(bf16[8,104,768]{2,1,0:T(8,128)(2,1)S(1)} %all_to_all.15.own_ref), channel_id=1, source_target_pairs={{8,16},{9,17},{10,18},{11,19},{12,20},{13,21},{14,22},{15,23},{16,... | collective-permute-start | bytes 3833864 | tf_op jit(solution)/shard_map/ppermute | solution.py:258
  34.4 17.7 %collective-permute-start = (bf16[8,104,768]{2,1,0:T(8,128)(2,1)S(1)}, bf16[8,104,768]{2,1,0:T(8,128)(2,1)}, u32[]{:S(2)}, u32[]{:S(2)}) collective-permute-start(bf16[8,104,768]{2,1,0:T(8,128)(2,1)S(1)} %all_to_all.15.own_ref), channel_id=1, source_target_pairs={{0,8},{1,9},{2,10},{3,11},{4,12},{5,13},{6,14},{7,15},{8,0},{9,1},... | collective-permute-start | bytes 3833864 | tf_op jit(solution)/shard_map/ppermute | solution.py:258
  36.3 15.8 %all-to-all-start = ((bf16[8,104,384]{2,1,0:T(8,128)(2,1)}), bf16[8,104,384]{2,1,0:T(8,128)(2,1)S(1)}, u32[]{:S(2)}, u32[]{:S(2)}) async-start(bf16[8,104,384]{2,1,0:T(8,128)(2,1)} %copy-done.1), calls=%async_computation | async-start | bytes 1277952 | tf_op jit(solution)/shard_map/all_to_all | solution.py:262

commit v3 on v2

--- a/solution.py
+++ b/solution.py
@@ -15,7 +15,7 @@
 BLOCK_COLS = 2
 MOST_COLS = 2
 SCALE = 1.4426950408889634 / HEAD_DIM**0.5
-VMEM_LIMIT = 32 * 2**20
+ORDER_FLOPS = 2 * 10**10
 
 
 def geometry(tokens):
@@ -27,8 +27,8 @@
     return -(-rows // 8) * 8
 
 
-def params():
-    return pltpu.CompilerParams(vmem_limit_bytes=VMEM_LIMIT)
+def params(mib):
+    return pltpu.CompilerParams(vmem_limit_bytes=mib * 2**20)
 
 
 def in_smem():
@@ -45,12 +45,11 @@
     groups, slot_rows, width = q_out.shape
     rows = k_ref.shape[0]
     heads = width // HEAD_DIM
-    places = ((kv_out, 0), (kv_out, width), (q_out, 0))
     copies = [
         pltpu.make_async_copy(source, scale_buf.at[at], sems.at[at])
         for at, source in enumerate((ks_ref, vs_ref, qs_ref))
     ] + [
-        pltpu.make_async_copy(source, buf.at[at], sems.at[len(places) + at])
+        pltpu.make_async_copy(source, buf.at[at], sems.at[3 + at])
         for at, source in enumerate((k_ref, v_ref, q_ref))
     ]
     for copy in copies:
@@ -58,19 +57,25 @@
     for copy in copies:
         copy.wait()
     blank = jnp.zeros((slot_rows - rows, HEAD_DIM), jnp.float32)
-    for at, (out_ref, low) in enumerate(places):
-        scales = scale_buf[at].astype(jnp.float32).T
-        for group in range(groups):
-            for head in range(heads):
-                index = group * heads + head
-                vals = buf[at, :, index * HEAD_DIM : (index + 1) * HEAD_DIM]
-                wide = vals.astype(jnp.float32) * scales[:, index : index + 1]
-                if slot_rows > rows:
-                    wide = jnp.concatenate([wide, blank], 0)
-                start = low + head * HEAD_DIM
-                out_ref[group ^ flip_ref[0], :, start : start + HEAD_DIM] = wide.astype(
-                    jnp.bfloat16
-                )
+    scales = [scale_buf[at].astype(jnp.float32).T for at in range(3)]
+
+    def scaled(at, index):
+        vals = buf[at, :, index * HEAD_DIM : (index + 1) * HEAD_DIM]
+        return vals.astype(jnp.float32) * scales[at][:, index : index + 1]
+
+    for group in range(groups):
+        indices = range(group * heads, (group + 1) * heads)
+        stacked = [scaled(at, index) for index in indices for at in range(2)]
+        slot = group ^ flip_ref[0]
+        kv_out[slot] = jnp.concatenate(stacked, 0).astype(jnp.bfloat16)
+    for group in range(groups):
+        slot = group ^ flip_ref[0]
+        for head in range(heads):
+            wide = scaled(2, group * heads + head)
+            if slot_rows > rows:
+                wide = jnp.concatenate([wide, blank], 0)
+            low = head * HEAD_DIM
+            q_out[slot, :, low : low + HEAD_DIM] = wide.astype(jnp.bfloat16)
 
 
 def pack(flip, k_vals, v_vals, q_vals, k_scale, v_scale, q_scale):
@@ -85,7 +90,7 @@
     return pl.pallas_call(
         pack_kernel,
         out_shape=(
-            jax.ShapeDtypeStruct((groups, slot_rows, 2 * width), jnp.bfloat16),
+            jax.ShapeDtypeStruct((groups, 2 * rows * (width // HEAD_DIM), HEAD_DIM), jnp.bfloat16),
             jax.ShapeDtypeStruct((groups, slot_rows, width), jnp.bfloat16),
         ),
         in_specs=[in_smem()] + [pl.BlockSpec(memory_space=pltpu.HBM)] * 6,
@@ -95,7 +100,7 @@
             pltpu.VMEM((3, k_scale.shape[1], rows), jnp.bfloat16),
             pltpu.SemaphoreType.DMA((6,)),
         ],
-        compiler_params=params(),
+        compiler_params=params(8),
     )(flip, *operands)
 
 
@@ -114,22 +119,47 @@
         out_shape=jax.ShapeDtypeStruct((rows, groups * width), jnp.bfloat16),
         in_specs=[in_smem(), in_vmem()],
         out_specs=in_vmem(),
-        compiler_params=params(),
+        compiler_params=params(4),
     )(flip, slots)
 
 
-def by_columns(slots_ref, lanes, lin_ref, chunk):
-    slots = slots_ref.shape[0]
-    rows, cols, _ = geometry(slots * chunk)
-    for slot in range(slots):
-        part = slots_ref[slot, :, lanes].astype(jnp.float32)
-        lin_ref[slot * chunk : slot * chunk + part.shape[0], :] = part
-    for col in range(cols):
-        pieces = []
-        for row in range(rows):
-            low = row * FRAME_W + col * TILE_W
-            pieces.append(lin_ref[low : low + TILE_W, :])
-        yield col, jnp.concatenate(pieces, 0)
+def tokens_by_eight(slots, base, chunk):
+    first_half = lax.broadcasted_iota(jnp.int32, (TILE_W, HEAD_DIM), 0) < TILE_W // 2
+    half = TILE_W // 2
+    turned = {}
+
+    def aligned(slot, low):
+        return slots[slot][low : low + TILE_W, :]
+
+    def halves_swapped(slot, low):
+        if (slot, low) not in turned:
+            turned[slot, low] = pltpu.roll(aligned(slot, low), half, 0)
+        return turned[slot, low]
+
+    def upper(slot, low):
+        return aligned(slot, low) if low % TILE_W == 0 else halves_swapped(slot, low - half)
+
+    def lower(slot, low):
+        return halves_swapped(slot, low) if low % TILE_W == 0 else aligned(slot, low - half)
+
+    def eight(slot, low):
+        if low % TILE_W == 0:
+            return aligned(slot, low)
+        return jnp.where(first_half, upper(slot, low), lower(slot, low + half))
+
+    full = chunk // TILE_W
+    for slot in range(0, len(slots), 2):
+        for at in range(full):
+            yield eight(slot, base + at * TILE_W)
+        yield jnp.where(first_half, upper(slot, base + full * TILE_W), lower(slot + 1, base))
+        for at in range(full):
+            yield eight(slot + 1, base + half + at * TILE_W)
+
+
+def by_columns(slots, base, chunk):
+    cols = FRAME_W // TILE_W
+    groups = list(tokens_by_eight(slots, base, chunk))
+    return [jnp.concatenate(groups[col::cols], 0) for col in range(cols)]
 
 
 def blocks(cols, strip, span):
@@ -166,8 +196,7 @@
 
 
 def attend_kernel(
-    meta_ref, q_ref, own_ref, beside_ref, away_ref, out_ref, lin_ref, qs_ref, ks_ref, vs_ref,
-    lin_out_ref, *, chunk,
+    meta_ref, q_ref, own_ref, beside_ref, away_ref, out_ref, qs_ref, ks_ref, vs_ref, lin_out_ref, *, chunk,
 ):
     slots, slot_rows, width = out_ref.shape
     heads = width // HEAD_DIM
@@ -175,27 +204,34 @@
     rows, cols, strip = geometry(tokens)
     sources = (own_ref, beside_ref, away_ref)
     span = len(sources)
-    vs_ref[:, HEAD_DIM:] = jnp.ones((vs_ref.shape[0], vs_ref.shape[1] - HEAD_DIM), vs_ref.dtype)
+    ones = jnp.ones((vs_ref.shape[1], vs_ref.shape[2] - HEAD_DIM), vs_ref.dtype)
+    for head in range(heads):
+        vs_ref[head, :, HEAD_DIM:] = ones
     lin_out_ref[tokens:, :] = jnp.zeros((lin_out_ref.shape[0] - tokens, HEAD_DIM), jnp.float32)
     away = jnp.where(meta_ref[3 * heads] > 0, 1.0, 2.0)
+
+    for frame, source in enumerate(sources):
+        taken = [source[slot].astype(jnp.float32) for slot in range(slots)]
+        for head in range(heads):
+            for at, target in enumerate((ks_ref, vs_ref)):
+                for col, part in enumerate(by_columns(taken, (2 * head + at) * chunk, chunk)):
+                    low = (col * span + frame) * strip
+                    target[head, low : low + strip, :HEAD_DIM] = part.astype(jnp.bfloat16)
+    for head in range(heads):
+        lanes = slice(head * HEAD_DIM, (head + 1) * HEAD_DIM)
+        taken = [q_ref[slot, :, lanes].astype(jnp.float32) for slot in range(slots)]
+        for col, part in enumerate(by_columns(taken, 0, chunk)):
+            qs_ref[head, col * strip : (col + 1) * strip, :] = part.astype(jnp.bfloat16)
 
     @pl.loop(0, heads)
     def _(head):
         lanes = pl.ds(pl.multiple_of(head * HEAD_DIM, HEAD_DIM), HEAD_DIM)
-        value_lanes = pl.ds(pl.multiple_of((heads + head) * HEAD_DIM, HEAD_DIM), HEAD_DIM)
-        for col, part in by_columns(q_ref, lanes, lin_ref, chunk):
-            qs_ref[col * strip : (col + 1) * strip, :] = part.astype(jnp.bfloat16)
-        for frame, source in enumerate(sources):
-            for take, target in ((lanes, ks_ref), (value_lanes, vs_ref)):
-                for col, part in by_columns(source, take, lin_ref, chunk):
-                    low = (col * span + frame) * strip
-                    target[low : low + strip, :HEAD_DIM] = part.astype(jnp.bfloat16)
         reach = [meta_ref[3 * head + i].astype(jnp.float32) for i in range(3)]
         all_blocks = blocks(cols, strip, span)
         all_scores = [
             lax.dot_general(
-                qs_ref[query, :],
-                ks_ref[key, :],
+                qs_ref[head, query, :],
+                ks_ref[head, key, :],
                 (((1,), (1,)), ((), ())),
                 preferred_element_type=jnp.float32,
             )
@@ -210,7 +246,7 @@
                 weights.append(jnp.exp2((masked - top) * SCALE))
             all_weights.append(jnp.concatenate(weights, 0).astype(jnp.bfloat16))
         for (start, _, _, key), weights in zip(all_blocks, all_weights):
-            sums = jnp.dot(weights, vs_ref[key, :], preferred_element_type=jnp.float32)
+            sums = jnp.dot(weights, vs_ref[head, key, :], preferred_element_type=jnp.float32)
             result = sums[:, :HEAD_DIM] / sums[:, HEAD_DIM:]
             for col in range(start, start + BLOCK_COLS):
                 for row in range(rows):
@@ -224,6 +260,7 @@
 
 def attend(meta, q, own, beside, away, chunk):
     slots, slot_rows, width = q.shape
+    heads = width // HEAD_DIM
     tokens = slots * chunk
     lin_rows = padded(tokens + slot_rows - chunk)
     return pl.pallas_call(
@@ -232,14 +269,29 @@
         in_specs=[in_smem()] + [in_vmem()] * 4,
         out_specs=in_vmem(),
         scratch_shapes=[
-            pltpu.VMEM((lin_rows, HEAD_DIM), jnp.float32),
-            pltpu.VMEM((tokens, HEAD_DIM), jnp.bfloat16),
-            pltpu.VMEM((3 * tokens, HEAD_DIM), jnp.bfloat16),
-            pltpu.VMEM((3 * tokens, 2 * HEAD_DIM), jnp.bfloat16),
+            pltpu.VMEM((heads, tokens, HEAD_DIM), jnp.bfloat16),
+            pltpu.VMEM((heads, 3 * tokens, HEAD_DIM), jnp.bfloat16),
+            pltpu.VMEM((heads, 3 * tokens, 2 * HEAD_DIM), jnp.bfloat16),
             pltpu.VMEM((lin_rows, HEAD_DIM), jnp.float32),
         ],
-        compiler_params=params(),
+        compiler_params=params(16),
     )(meta, q, own, beside, away)
+
+
+def after_kernel(meta_ref, array_ref, out_ref):
+    for at in range(meta_ref.shape[0]):
+        out_ref[at] = meta_ref[at]
+
+
+def after(meta, array):
+    return pl.pallas_call(
+        after_kernel,
+        out_shape=jax.ShapeDtypeStruct(meta.shape, meta.dtype),
+        in_specs=[in_smem(), pl.BlockSpec(memory_space=pl.ANY)],
+        out_specs=in_smem(),
+        compiler_params=params(1),
+        cost_estimate=pl.CostEstimate(flops=ORDER_FLOPS, bytes_accessed=0, transcendentals=0),
+    )(meta, array)
 
 
 def turn(slab, slabs, groups):
@@ -276,9 +328,10 @@
     meta = jnp.concatenate([reach.reshape(-1), linked.reshape(1)])
     kv, q = pack(flip, k_vals, v_vals, q_vals, k_scale, v_scale, q_scale)
     kv = swap(kv)
+    away = exchange(kv, [(s, s + 1) for s in range(1, slabs - 1, 2)])
     beside = exchange(kv, [(s, s + 1) for s in range(0, slabs, 2)])
-    away = exchange(kv, [(s, s + 1) for s in range(1, slabs - 1, 2)])
     q = swap(q)
+    meta = after(meta, away)
     attended = attend(meta, q, kv, beside, away, chunk)
     return unpack(flip, swap(attended), chunk)
 

time: 74.3 us -> 70.7 us (0.952)
  waiting for transfers between devices: 11.7 us -> 8.48 us
  blocking collectives: 36.9 us -> 35.2 us
  Pallas kernels: 10.4 us -> 11.7 us
    all_to_all x1, waiting for transfers between devices: 11.7 us -> 0.01 us  [swap(): return lax.all_to_all(slots, 'head', split_axis=0, concat_axis=0)]
    ppermute x2, waiting for transfers between devices: 0.01 us -> 8.47 us  [exchange(): return lax.ppermute(array, ('slab', 'head'), both)]
    all_to_all x2, blocking collectives: 36.9 us -> 35.2 us  [swap(): return lax.all_to_all(slots, 'head', split_axis=0, concat_axis=0)]
    pallas_call x1 -> x2, Pallas kernels: 2.5 us -> 3.49 us  [the longest x1 2.35 us: pack(): pl.pallas_call(pack_kernel, out_shape=(jax.ShapeDtypeStruct((groups, 2 *...]
  transfers between devices with their start and end apart: 3 -> 3, of which waited for: 1 -> 1; matrix products, arithmetic and copies ran while one was open for 0% -> 0% of each run, Pallas kernels for 0% -> 2%
where the time goes in v3:
time: 70.7 us; the launch traced here: 70.4 us
  blocking collectives  35.2 us (50%)
  starting transfers between devices  14.6 us (21%)
  Pallas kernels  11.7 us (17%)
  waiting for transfers between devices  8.48 us (12%)
    all_to_all x2, blocking collectives, swap(): return lax.all_to_all(slots, 'head', split_axis=0, concat_axis=0)  35.2 us
    ppermute x2, starting transfers between devices, exchange(): return lax.ppermute(array, ('slab', 'head'), both)  10.9 us
    ppermute x2, waiting for transfers between devices, exchange(): return lax.ppermute(array, ('slab', 'head'), both)  8.47 us
    pallas_call x1, Pallas kernels, attend(): pl.pallas_call(functools.partial(attend_kernel, chunk=chunk), out_shape=j...  7.28 us
    all_to_all x1, starting transfers between devices, swap(): return lax.all_to_all(slots, 'head', split_axis=0, concat_axis=0)  3.67 us
    pallas_call x1, Pallas kernels, pack(): pl.pallas_call(pack_kernel, out_shape=(jax.ShapeDtypeStruct((groups, 2 *...  2.35 us
  transfers between devices with their start and end apart: 3, of which 1 were waited for; matrix products, arithmetic and copies ran while one was open for 0% of the time, Pallas kernels for 2%

profile of v3, /device:TPU:16, one launch (start us, length us, event | category | flops | bytes accessed | tf_op | source)
XLA Modules:
  0.0 70.4 jit_solution(3361959906620934426)
XLA Ops:
  0.0 0.0 copy-start
  0.0 2.4 %shard_map.73 = (bf16[8,600,128]{2,1,0:T(8,128)(2,1)S(1)}, bf16[8,104,384]{2,1,0:T(8,128)(2,1)S(1)}) custom-call(s32[1]{0:T(128)} %bitcast.flip_ref, bf16[100,3072]{1,0:T(8,128)(2,1)} %k_ref.1, bf16[100,3072]{1,0:T(8,128)(2,1)} %v_ref.1, bf16[100,3072]{1,0:T(8,128)(2,1)} %q_ref.1, bf16[24,100]{1,0:T(8,128)(2,1)} %bitcast.5, bf16[24,100]{1,0:T(8,128)(2,1)} %bitcast.6, ...), custom_call_target="tpu_custom_call" | custom-call | tf_op jit(solution)/shard_map/pallas_call | solution.py:90
  2.4 0.0 copy-start.1
  2.4 22.4 %all_to_all.15.own_ref = bf16[8,600,128]{2,1,0:T(8,128)(2,1)S(1)} all-to-all(bf16[8,600,128]{2,1,0:T(8,128)(2,1)S(1)} %get-tuple-element.7), channel_id=1, replica_groups=mesh['slab'=64,'head'=8] {'head'}, dimensions={0} | all-to-all | bytes 2457600 | tf_op jit(solution)/shard_map/all_to_all | solution.py:314
  24.8 0.0 copy-done.1
  24.8 9.0 %collective-permute-start = (bf16[8,600,128]{2,1,0:T(8,128)(2,1)S(1)}, bf16[8,600,128]{2,1,0:T(8,128)(2,1)S(1)}, u32[]{:S(2)}, u32[]{:S(2)}) collective-permute-start(bf16[8,600,128]{2,1,0:T(8,128)(2,1)S(1)} %all_to_all.15.own_ref), channel_id=1, source_target_pairs={{8,16},{9,17},{10,18},{11,19},{12,20},{13,21},{14,22},{15,23},{16,... | collective-permute-start | bytes 3686408 | tf_op jit(solution)/shard_map/ppermute | solution.py:310
  33.9 3.7 %all-to-all-start.1 = ((bf16[8,104,384]{2,1,0:T(8,128)(2,1)}), bf16[8,104,384]{2,1,0:T(8,128)(2,1)S(1)}, u32[]{:S(2)}, u32[]{:S(2)}) async-start(bf16[8,104,384]{2,1,0:T(8,128)(2,1)} %copy-done.1), calls=%async_computation.1 | async-start | bytes 1277952 | tf_op jit(solution)/shard_map/all_to_all | solution.py:314
  37.5 0.0 copy-done
  37.5 0.1 constant_dynamic-slice_fusion
  37.6 0.1 copy.8
  37.7 0.1 reshape.13
  37.8 0.1 pad_add_fusion.meta_ref
  37.9 1.9 %collective-permute-start.1 = (bf16[8,600,128]{2,1,0:T(8,128)(2,1)S(1)}, bf16[8,600,128]{2,1,0:T(8,128)(2,1)}, u32[]{:S(2)}, u32[]{:S(2)}) collective-permute-start(bf16[8,600,128]{2,1,0:T(8,128)(2,1)S(1)} %all_to_all.15.own_ref), channel_id=1, source_target_pairs={{0,8},{1,9},{2,10},{3,11},{4,12},{5,13},{6,14},{7,15},{8,0},{9,1},... | collective-permute-start | bytes 3686408 | tf_op jit(solution)/shard_map/ppermute | solution.py:310
  39.8 8.5 %collective-permute-done.array_ref.away_ref = bf16[8,600,128]{2,1,0:T(8,128)(2,1)S(1)} collective-permute-done((bf16[8,600,128]{2,1,0:T(8,128)(2,1)S(1)}, bf16[8,600,128]{2,1,0:T(8,128)(2,1)S(1)}, u32[]{:S(2)}, u32[]{:S(2)}) %collective-permute-start) | collective-permute-done | bytes 1228832 | tf_op jit(solution)/shard_map/ppermute | solution.py:310
  48.3 1.1 %shard_map.74.meta_ref = s32[10]{0:T(128)S(1)} custom-call(s32[10]{0:T(128)S(1)} %pad_add_fusion.meta_ref, bf16[8,600,128]{2,1,0:T(8,128)(2,1)S(1)} %collective-permute-done.array_ref.away_ref), custom_call_target="tpu_custom_call" | custom-call | flops 20000000000 | tf_op jit(solution)/shard_map/pallas_call | solution.py:287
  49.4 0.0 all-to-all-done.1.q_ref
  49.4 0.0 collective-permute-done.1.beside_ref
  49.4 7.3 %shard_map.75 = bf16[8,104,384]{2,1,0:T(8,128)(2,1)S(1)} custom-call(s32[10]{0:T(128)S(1)} %shard_map.74.meta_ref, bf16[8,104,384]{2,1,0:T(8,128)(2,1)S(1)} %all-to-all-done.1.q_ref, bf16[8,600,128]{2,1,0:T(8,128)(2,1)S(1)} %all_to_all.15.own_ref, bf16[8,600,128]{2,1,0:T(8,128)(2,1)} %collective-permute-done.1.beside_ref, ...), custom_call_target="tpu_custom_call" | custom-call | tf_op jit(solution)/shard_map/pallas_call | solution.py:266
  56.7 12.8 %all_to_all.16.in_ref = bf16[8,104,384]{2,1,0:T(8,128)(2,1)S(1)} all-to-all(bf16[8,104,384]{2,1,0:T(8,128)(2,1)S(1)} %shard_map.75), channel_id=1, replica_groups=mesh['slab'=64,'head'=8] {'head'}, dimensions={0} | all-to-all | bytes 1277952 | tf_op jit(solution)/shard_map/all_to_all | solution.py:314
  69.5 0.9 %shard_map.76 = bf16[100,3072]{1,0:T(8,128)(2,1)} custom-call(s32[1]{0:T(128)} %bitcast.flip_ref, bf16[8,104,384]{2,1,0:T(8,128)(2,1)S(1)} %all_to_all.16.in_ref), custom_call_target="tpu_custom_call" | custom-call | tf_op jit(solution)/shard_map/pallas_call | solution.py:117
Async XLA Ops:
  0.0 37.5 %copy-start = (s32[24,3]{0,1:T(4,128)S(1)}, s32[24,3]{0,1:T(4,128)}, u32[]{:S(2)}) copy-start(s32[24,3]{0,1:T(4,128)} %param.13) | copy-start | bytes 868
  2.4 22.5 %copy-start.1 = (bf16[8,104,384]{2,1,0:T(8,128)(2,1)}, bf16[8,104,384]{2,1,0:T(8,128)(2,1)S(1)}, u32[]{:S(2)}) copy-start(bf16[8,104,384]{2,1,0:T(8,128)(2,1)S(1)} %get-tuple-element.8) | copy-start | bytes 1916932
  24.8 23.4 %collective-permute-start = (bf16[8,600,128]{2,1,0:T(8,128)(2,1)S(1)}, bf16[8,600,128]{2,1,0:T(8,128)(2,1)S(1)}, u32[]{:S(2)}, u32[]{:S(2)}) collective-permute-start(bf16[8,600,128]{2,1,0:T(8,128)(2,1)S(1)} %all_to_all.15.own_ref), channel_id=1, source_target_pairs={{8,16},{9,17},{10,18},{11,19},{12,20},{13,21},{14,22},{15,23},{16,... | collective-permute-start | bytes 3686408 | tf_op jit(solution)/shard_map/ppermute | solution.py:310
  33.9 15.6 %all-to-all-start.1 = ((bf16[8,104,384]{2,1,0:T(8,128)(2,1)}), bf16[8,104,384]{2,1,0:T(8,128)(2,1)S(1)}, u32[]{:S(2)}, u32[]{:S(2)}) async-start(bf16[8,104,384]{2,1,0:T(8,128)(2,1)} %copy-done.1), calls=%async_computation.1 | async-start | bytes 1277952 | tf_op jit(solution)/shard_map/all_to_all | solution.py:314
  37.9 11.6 %collective-permute-start.1 = (bf16[8,600,128]{2,1,0:T(8,128)(2,1)S(1)}, bf16[8,600,128]{2,1,0:T(8,128)(2,1)}, u32[]{:S(2)}, u32[]{:S(2)}) collective-permute-start(bf16[8,600,128]{2,1,0:T(8,128)(2,1)S(1)} %all_to_all.15.own_ref), channel_id=1, source_target_pairs={{0,8},{1,9},{2,10},{3,11},{4,12},{5,13},{6,14},{7,15},{8,0},{9,1},... | collective-permute-start | bytes 3686408 | tf_op jit(solution)/shard_map/ppermute | solution.py:310

commit v4 on v3

--- a/solution.py
+++ b/solution.py
@@ -162,22 +162,17 @@
     return [jnp.concatenate(groups[col::cols], 0) for col in range(cols)]
 
 
-def blocks(cols, strip, span):
-    found = []
+def blocks(cols, reach):
     for start in range(0, cols, BLOCK_COLS):
-        low = max(0, start - MOST_COLS)
-        high = min(cols, start + BLOCK_COLS + MOST_COLS)
-        query = slice(start * strip, (start + BLOCK_COLS) * strip)
-        key = slice(low * span * strip, high * span * strip)
-        found.append((start, low, query, key))
-    return found
+        yield start, max(0, start - reach), min(cols, start + BLOCK_COLS + reach)
 
 
 def shifts(block, strip, rows, frames, frame_reach, row_reach, col_reach):
-    start, low_col, _, key = block
+    start, low_col, high_col = block
     span = len(frames)
     half = strip * TILE_H // rows
-    at = lax.broadcasted_iota(jnp.int32, (1, key.stop - key.start), 1).astype(jnp.float32)
+    keys = (high_col - low_col) * span * strip
+    at = lax.broadcasted_iota(jnp.int32, (1, keys), 1).astype(jnp.float32)
     key_col = jnp.floor((at + 0.5) * (1.0 / (span * strip)))
     rest = at - key_col * (span * strip)
     key_frame = jnp.floor((rest + 0.5) * (1.0 / strip))
@@ -196,102 +191,140 @@
 
 
 def attend_kernel(
-    meta_ref, q_ref, own_ref, beside_ref, away_ref, out_ref, qs_ref, ks_ref, vs_ref, lin_out_ref, *, chunk,
+    zeros_ref, meta_ref, q_ref, own_ref, away_ref, beside_hbm, out_ref, qs_ref, ks_ref, vs_ref, lin_out_ref,
+    beside_ref, sem, *, chunk,
 ):
     slots, slot_rows, width = out_ref.shape
     heads = width // HEAD_DIM
     tokens = slots * chunk
     rows, cols, strip = geometry(tokens)
-    sources = (own_ref, beside_ref, away_ref)
-    span = len(sources)
+    span = 3
+    copy = pltpu.make_async_copy(beside_hbm, beside_ref, sem)
+    copy.start()
     ones = jnp.ones((vs_ref.shape[1], vs_ref.shape[2] - HEAD_DIM), vs_ref.dtype)
     for head in range(heads):
         vs_ref[head, :, HEAD_DIM:] = ones
-    lin_out_ref[tokens:, :] = jnp.zeros((lin_out_ref.shape[0] - tokens, HEAD_DIM), jnp.float32)
+    lin_out_ref[tokens:, :] = zeros_ref[: lin_out_ref.shape[0] - tokens, :]
     away = jnp.where(meta_ref[3 * heads] > 0, 1.0, 2.0)
 
-    for frame, source in enumerate(sources):
-        taken = [source[slot].astype(jnp.float32) for slot in range(slots)]
-        for head in range(heads):
-            for at, target in enumerate((ks_ref, vs_ref)):
-                for col, part in enumerate(by_columns(taken, (2 * head + at) * chunk, chunk)):
-                    low = (col * span + frame) * strip
-                    target[head, low : low + strip, :HEAD_DIM] = part.astype(jnp.bfloat16)
     for head in range(heads):
         lanes = slice(head * HEAD_DIM, (head + 1) * HEAD_DIM)
         taken = [q_ref[slot, :, lanes].astype(jnp.float32) for slot in range(slots)]
         for col, part in enumerate(by_columns(taken, 0, chunk)):
             qs_ref[head, col * strip : (col + 1) * strip, :] = part.astype(jnp.bfloat16)
 
-    @pl.loop(0, heads)
-    def _(head):
-        lanes = pl.ds(pl.multiple_of(head * HEAD_DIM, HEAD_DIM), HEAD_DIM)
+    def by_head(frame, source, head):
+        taken = [source[slot].astype(jnp.float32) for slot in range(slots)]
+        for at, target in enumerate((ks_ref, vs_ref)):
+            for col, part in enumerate(by_columns(taken, (2 * head + at) * chunk, chunk)):
+                low = (col * span + frame) * strip
+                target[head, low : low + strip, :HEAD_DIM] = part.astype(jnp.bfloat16)
+
+    for head in range(heads):
+        by_head(0, own_ref, head)
+    copy.wait()
+    for head in range(heads):
+
+        @pl.when(meta_ref[3 * head] > 0)
+        def _(head=head):
+            by_head(1, beside_ref, head)
+            by_head(2, away_ref, head)
+
+    def columns(ref, head, low, high, frames):
+        if len(frames) == span:
+            return ref[head, low * span * strip : high * span * strip, :]
+        first = [col * span * strip for col in range(low, high)]
+        return jnp.concatenate([ref[head, at : at + strip, :] for at in first], 0)
+
+    def one_head(head, frames, most_cols):
         reach = [meta_ref[3 * head + i].astype(jnp.float32) for i in range(3)]
-        all_blocks = blocks(cols, strip, span)
+        all_blocks = list(blocks(cols, most_cols))
         all_scores = [
             lax.dot_general(
-                qs_ref[head, query, :],
-                ks_ref[head, key, :],
+                qs_ref[head, start * strip : (start + BLOCK_COLS) * strip, :],
+                columns(ks_ref, head, low, high, frames),
                 (((1,), (1,)), ((), ())),
                 preferred_element_type=jnp.float32,
             )
-            for _, _, query, key in all_blocks
+            for start, low, high in all_blocks
         ]
         all_weights = []
         for block, scores in zip(all_blocks, all_scores):
             weights = []
-            for mine, shift in shifts(block, strip, rows, (0.0, 1.0, away), *reach):
+            for mine, shift in shifts(block, strip, rows, frames, *reach):
                 masked = scores[mine, :] + shift
                 top = jnp.max(masked, axis=1, keepdims=True)
                 weights.append(jnp.exp2((masked - top) * SCALE))
             all_weights.append(jnp.concatenate(weights, 0).astype(jnp.bfloat16))
-        for (start, _, _, key), weights in zip(all_blocks, all_weights):
-            sums = jnp.dot(weights, vs_ref[head, key, :], preferred_element_type=jnp.float32)
+        for (start, low, high), weights in zip(all_blocks, all_weights):
+            values = columns(vs_ref, head, low, high, frames)
+            sums = jnp.dot(weights, values, preferred_element_type=jnp.float32)
             result = sums[:, :HEAD_DIM] / sums[:, HEAD_DIM:]
             for col in range(start, start + BLOCK_COLS):
                 for row in range(rows):
-                    low = row * FRAME_W + col * TILE_W
+                    low_row = row * FRAME_W + col * TILE_W
                     got = (col - start) * strip + row * TILE_W
-                    lin_out_ref[low : low + TILE_W, :] = result[got : got + TILE_W, :]
+                    lin_out_ref[low_row : low_row + TILE_W, :] = result[got : got + TILE_W, :]
+
+    @pl.loop(0, heads)
+    def _(head):
+        more_frames = meta_ref[3 * head] > 0
+        most = meta_ref[3 * head + 2] >= MOST_COLS
+
+        @pl.when(more_frames & most)
+        def _():
+            one_head(head, (0.0, 1.0, away), MOST_COLS)
+
+        @pl.when(more_frames & jnp.logical_not(most))
+        def _():
+            one_head(head, (0.0, 1.0, away), MOST_COLS - 1)
+
+        @pl.when(jnp.logical_not(more_frames))
+        def _():
+            one_head(head, (0.0,), MOST_COLS)
+
+        lanes = pl.ds(pl.multiple_of(head * HEAD_DIM, HEAD_DIM), HEAD_DIM)
         for slot in range(slots):
             low = slot * chunk
             out_ref[slot, :, lanes] = lin_out_ref[low : low + slot_rows, :].astype(jnp.bfloat16)
 
 
-def attend(meta, q, own, beside, away, chunk):
+def attend(zeros, meta, q, own, beside, away, chunk):
     slots, slot_rows, width = q.shape
     heads = width // HEAD_DIM
     tokens = slots * chunk
     lin_rows = padded(tokens + slot_rows - chunk)
+    hbm = pl.BlockSpec(memory_space=pltpu.HBM)
     return pl.pallas_call(
         functools.partial(attend_kernel, chunk=chunk),
         out_shape=jax.ShapeDtypeStruct(q.shape, jnp.bfloat16),
-        in_specs=[in_smem()] + [in_vmem()] * 4,
+        in_specs=[in_vmem(), in_smem()] + [in_vmem()] * 3 + [hbm],
         out_specs=in_vmem(),
         scratch_shapes=[
             pltpu.VMEM((heads, tokens, HEAD_DIM), jnp.bfloat16),
             pltpu.VMEM((heads, 3 * tokens, HEAD_DIM), jnp.bfloat16),
             pltpu.VMEM((heads, 3 * tokens, 2 * HEAD_DIM), jnp.bfloat16),
             pltpu.VMEM((lin_rows, HEAD_DIM), jnp.float32),
+            pltpu.VMEM(beside.shape, beside.dtype),
+            pltpu.SemaphoreType.DMA,
         ],
         compiler_params=params(16),
-    )(meta, q, own, beside, away)
-
-
-def after_kernel(meta_ref, array_ref, out_ref):
-    for at in range(meta_ref.shape[0]):
-        out_ref[at] = meta_ref[at]
-
-
-def after(meta, array):
+    )(zeros, meta, q, own, away, pltpu.with_memory_space_constraint(beside, pltpu.HBM))
+
+
+def after_kernel(array_ref, out_ref):
+    out_ref[...] = jnp.zeros_like(out_ref)
+
+
+def after(array):
     return pl.pallas_call(
         after_kernel,
-        out_shape=jax.ShapeDtypeStruct(meta.shape, meta.dtype),
-        in_specs=[in_smem(), pl.BlockSpec(memory_space=pl.ANY)],
-        out_specs=in_smem(),
+        out_shape=jax.ShapeDtypeStruct((8, HEAD_DIM), jnp.float32),
+        in_specs=[pl.BlockSpec(memory_space=pl.ANY)],
+        out_specs=in_vmem(),
         compiler_params=params(1),
         cost_estimate=pl.CostEstimate(flops=ORDER_FLOPS, bytes_accessed=0, transcendentals=0),
-    )(meta, array)
+    )(array)
 
 
 def turn(slab, slabs, groups):
@@ -331,8 +364,7 @@
     away = exchange(kv, [(s, s + 1) for s in range(1, slabs - 1, 2)])
     beside = exchange(kv, [(s, s + 1) for s in range(0, slabs, 2)])
     q = swap(q)
-    meta = after(meta, away)
-    attended = attend(meta, q, kv, beside, away, chunk)
+    attended = attend(after(away), meta, q, kv, beside, away, chunk)
     return unpack(flip, swap(attended), chunk)
 
 

time: 70.7 us -> 68.3 us (0.966)
  Pallas kernels: 11.7 us -> 8.15 us
  blocking collectives: 35.2 us -> 36.3 us
    pallas_call x1, Pallas kernels: 7.28 us -> 4.91 us  [attend(): pl.pallas_call(functools.partial(attend_kernel, chunk=chunk), out_shape=j...]
    pallas_call x1, Pallas kernels: 1.14 us -> 0.01 us  [after(): pl.pallas_call(after_kernel, out_shape=jax.ShapeDtypeStruct((8, HEAD_DIM)...]
    all_to_all x2, blocking collectives: 35.2 us -> 36.3 us  [swap(): return lax.all_to_all(slots, 'head', split_axis=0, concat_axis=0)]
  transfers between devices with their start and end apart: 3 -> 3, of which waited for: 1 -> 1; matrix products, arithmetic and copies ran while one was open for 0% -> 0% of each run, Pallas kernels for 2% -> 0%
where the time goes in v4:
time: 68.3 us; the launch traced here: 67.9 us
  blocking collectives  36.3 us (53%)
  starting transfers between devices  14.6 us (21%)
  waiting for transfers between devices  8.48 us (12%)
  Pallas kernels  8.15 us (12%)
    all_to_all x2, blocking collectives, swap(): return lax.all_to_all(slots, 'head', split_axis=0, concat_axis=0)  36.3 us
    ppermute x2, starting transfers between devices, exchange(): return lax.ppermute(array, ('slab', 'head'), both)  10.9 us
    ppermute x2, waiting for transfers between devices, exchange(): return lax.ppermute(array, ('slab', 'head'), both)  8.47 us
    pallas_call x1, Pallas kernels, attend(): pl.pallas_call(functools.partial(attend_kernel, chunk=chunk), out_shape=j...  4.91 us
    all_to_all x1, starting transfers between devices, swap(): return lax.all_to_all(slots, 'head', split_axis=0, concat_axis=0)  3.67 us
    pallas_call x1, Pallas kernels, pack(): pl.pallas_call(pack_kernel, out_shape=(jax.ShapeDtypeStruct((groups, 2 *...  2.35 us
  transfers between devices with their start and end apart: 3, of which 1 were waited for; matrix products, arithmetic and copies ran while one was open for 0% of the time, Pallas kernels for 0%

profile of v4, /device:TPU:16, one launch (start us, length us, event | category | flops | bytes accessed | tf_op | source)
XLA Modules:
  0.0 67.9 jit_solution(18182046401779779560)
XLA Ops:
  0.0 0.0 copy-start
  0.0 2.4 %shard_map.73 = (bf16[8,600,128]{2,1,0:T(8,128)(2,1)S(1)}, bf16[8,104,384]{2,1,0:T(8,128)(2,1)S(1)}) custom-call(s32[1]{0:T(128)} %bitcast.flip_ref, bf16[100,3072]{1,0:T(8,128)(2,1)} %k_ref.1, bf16[100,3072]{1,0:T(8,128)(2,1)} %v_ref.1, bf16[100,3072]{1,0:T(8,128)(2,1)} %q_ref.1, bf16[24,100]{1,0:T(8,128)(2,1)} %bitcast.5, bf16[24,100]{1,0:T(8,128)(2,1)} %bitcast.6, ...), custom_call_target="tpu_custom_call" | custom-call | tf_op jit(solution)/shard_map/pallas_call | solution.py:90
  2.4 0.0 copy-start.1
  2.4 22.4 %all_to_all.15.own_ref = bf16[8,600,128]{2,1,0:T(8,128)(2,1)S(1)} all-to-all(bf16[8,600,128]{2,1,0:T(8,128)(2,1)S(1)} %get-tuple-element.7), channel_id=1, replica_groups=mesh['slab'=64,'head'=8] {'head'}, dimensions={0} | all-to-all | bytes 2457600 | tf_op jit(solution)/shard_map/all_to_all | solution.py:347
  24.8 0.0 copy-done.1
  24.8 9.0 %collective-permute-start = (bf16[8,600,128]{2,1,0:T(8,128)(2,1)S(1)}, bf16[8,600,128]{2,1,0:T(8,128)(2,1)S(1)}, u32[]{:S(2)}, u32[]{:S(2)}) collective-permute-start(bf16[8,600,128]{2,1,0:T(8,128)(2,1)S(1)} %all_to_all.15.own_ref), channel_id=1, source_target_pairs={{8,16},{9,17},{10,18},{11,19},{12,20},{13,21},{14,22},{15,23},{16,... | collective-permute-start | bytes 3686408 | tf_op jit(solution)/shard_map/ppermute | solution.py:343
  33.9 3.7 %all-to-all-start.1 = ((bf16[8,104,384]{2,1,0:T(8,128)(2,1)}), bf16[8,104,384]{2,1,0:T(8,128)(2,1)S(1)}, u32[]{:S(2)}, u32[]{:S(2)}) async-start(bf16[8,104,384]{2,1,0:T(8,128)(2,1)} %copy-done.1), calls=%async_computation.1 | async-start | bytes 1277952 | tf_op jit(solution)/shard_map/all_to_all | solution.py:347
  37.5 0.0 copy-done
  37.5 0.1 constant_dynamic-slice_fusion
  37.6 0.1 copy.8
  37.7 0.1 reshape.13
  37.8 0.1 pad_add_fusion.meta_ref
  37.9 1.9 %collective-permute-start.1 = (bf16[8,600,128]{2,1,0:T(8,128)(2,1)S(1)}, bf16[8,600,128]{2,1,0:T(8,128)(2,1)}, u32[]{:S(2)}, u32[]{:S(2)}) collective-permute-start(bf16[8,600,128]{2,1,0:T(8,128)(2,1)S(1)} %all_to_all.15.own_ref), channel_id=1, source_target_pairs={{0,8},{1,9},{2,10},{3,11},{4,12},{5,13},{6,14},{7,15},{8,0},{9,1},... | collective-permute-start | bytes 3686408 | tf_op jit(solution)/shard_map/ppermute | solution.py:343
  39.8 8.5 %collective-permute-done.array_ref.away_ref = bf16[8,600,128]{2,1,0:T(8,128)(2,1)S(1)} collective-permute-done((bf16[8,600,128]{2,1,0:T(8,128)(2,1)S(1)}, bf16[8,600,128]{2,1,0:T(8,128)(2,1)S(1)}, u32[]{:S(2)}, u32[]{:S(2)}) %collective-permute-start) | collective-permute-done | bytes 1228832 | tf_op jit(solution)/shard_map/ppermute | solution.py:343
  48.3 0.0 all-to-all-done.1.q_ref
  48.3 0.0 collective-permute-done.1.beside_hbm
  48.3 4.9 %shard_map.75 = bf16[8,104,384]{2,1,0:T(8,128)(2,1)S(1)} custom-call(f32[8,128]{1,0:T(8,128)S(1)} %shard_map.74.zeros_ref, s32[10]{0:T(128)S(1)} %pad_add_fusion.meta_ref, bf16[8,104,384]{2,1,0:T(8,128)(2,1)S(1)} %all-to-all-done.1.q_ref, bf16[8,600,128]{2,1,0:T(8,128)(2,1)S(1)} %all_to_all.15.own_ref, ...), custom_call_target="tpu_custom_call" | custom-call | tf_op jit(solution)/shard_map/pallas_call | solution.py:298
  53.2 13.9 %all_to_all.16.in_ref = bf16[8,104,384]{2,1,0:T(8,128)(2,1)S(1)} all-to-all(bf16[8,104,384]{2,1,0:T(8,128)(2,1)S(1)} %shard_map.75), channel_id=1, replica_groups=mesh['slab'=64,'head'=8] {'head'}, dimensions={0} | all-to-all | bytes 1277952 | tf_op jit(solution)/shard_map/all_to_all | solution.py:347
  67.1 0.9 %shard_map.76 = bf16[100,3072]{1,0:T(8,128)(2,1)} custom-call(s32[1]{0:T(128)} %bitcast.flip_ref, bf16[8,104,384]{2,1,0:T(8,128)(2,1)S(1)} %all_to_all.16.in_ref), custom_call_target="tpu_custom_call" | custom-call | tf_op jit(solution)/shard_map/pallas_call | solution.py:117
  (1 shorter events, 0.0 us)
Async XLA Ops:
  0.0 37.5 %copy-start = (s32[24,3]{0,1:T(4,128)S(1)}, s32[24,3]{0,1:T(4,128)}, u32[]{:S(2)}) copy-start(s32[24,3]{0,1:T(4,128)} %param.13) | copy-start | bytes 868
  2.4 22.5 %copy-start.1 = (bf16[8,104,384]{2,1,0:T(8,128)(2,1)}, bf16[8,104,384]{2,1,0:T(8,128)(2,1)S(1)}, u32[]{:S(2)}) copy-start(bf16[8,104,384]{2,1,0:T(8,128)(2,1)S(1)} %get-tuple-element.8) | copy-start | bytes 1916932
  24.8 23.4 %collective-permute-start = (bf16[8,600,128]{2,1,0:T(8,128)(2,1)S(1)}, bf16[8,600,128]{2,1,0:T(8,128)(2,1)S(1)}, u32[]{:S(2)}, u32[]{:S(2)}) collective-permute-start(bf16[8,600,128]{2,1,0:T(8,128)(2,1)S(1)} %all_to_all.15.own_ref), channel_id=1, source_target_pairs={{8,16},{9,17},{10,18},{11,19},{12,20},{13,21},{14,22},{15,23},{16,... | collective-permute-start | bytes 3686408 | tf_op jit(solution)/shard_map/ppermute | solution.py:343
  33.9 14.4 %all-to-all-start.1 = ((bf16[8,104,384]{2,1,0:T(8,128)(2,1)}), bf16[8,104,384]{2,1,0:T(8,128)(2,1)S(1)}, u32[]{:S(2)}, u32[]{:S(2)}) async-start(bf16[8,104,384]{2,1,0:T(8,128)(2,1)} %copy-done.1), calls=%async_computation.1 | async-start | bytes 1277952 | tf_op jit(solution)/shard_map/all_to_all | solution.py:347
  37.9 10.4 %collective-permute-start.1 = (bf16[8,600,128]{2,1,0:T(8,128)(2,1)S(1)}, bf16[8,600,128]{2,1,0:T(8,128)(2,1)}, u32[]{:S(2)}, u32[]{:S(2)}) collective-permute-start(bf16[8,600,128]{2,1,0:T(8,128)(2,1)S(1)} %all_to_all.15.own_ref), channel_id=1, source_target_pairs={{0,8},{1,9},{2,10},{3,11},{4,12},{5,13},{6,14},{7,15},{8,0},{9,1},... | collective-permute-start | bytes 3686408 | tf_op jit(solution)/shard_map/ppermute | solution.py:343

commit v5 on v4

--- a/solution.py
+++ b/solution.py
@@ -48,13 +48,14 @@
     copies = [
         pltpu.make_async_copy(source, scale_buf.at[at], sems.at[at])
         for at, source in enumerate((ks_ref, vs_ref, qs_ref))
-    ] + [
+    ]
+    copies += [
         pltpu.make_async_copy(source, buf.at[at], sems.at[3 + at])
         for at, source in enumerate((k_ref, v_ref, q_ref))
     ]
     for copy in copies:
         copy.start()
-    for copy in copies:
+    for copy in copies[:-1]:
         copy.wait()
     blank = jnp.zeros((slot_rows - rows, HEAD_DIM), jnp.float32)
     scales = [scale_buf[at].astype(jnp.float32).T for at in range(3)]
@@ -68,6 +69,7 @@
         stacked = [scaled(at, index) for index in indices for at in range(2)]
         slot = group ^ flip_ref[0]
         kv_out[slot] = jnp.concatenate(stacked, 0).astype(jnp.bfloat16)
+    copies[-1].wait()
     for group in range(groups):
         slot = group ^ flip_ref[0]
         for head in range(heads):
@@ -201,9 +203,6 @@
     span = 3
     copy = pltpu.make_async_copy(beside_hbm, beside_ref, sem)
     copy.start()
-    ones = jnp.ones((vs_ref.shape[1], vs_ref.shape[2] - HEAD_DIM), vs_ref.dtype)
-    for head in range(heads):
-        vs_ref[head, :, HEAD_DIM:] = ones
     lin_out_ref[tokens:, :] = zeros_ref[: lin_out_ref.shape[0] - tokens, :]
     away = jnp.where(meta_ref[3 * heads] > 0, 1.0, 2.0)
 
@@ -222,13 +221,14 @@
 
     for head in range(heads):
         by_head(0, own_ref, head)
-    copy.wait()
-    for head in range(heads):
-
-        @pl.when(meta_ref[3 * head] > 0)
-        def _(head=head):
-            by_head(1, beside_ref, head)
-            by_head(2, away_ref, head)
+    for frame, source in ((2, away_ref), (1, beside_ref)):
+        if source is beside_ref:
+            copy.wait()
+        for head in range(heads):
+
+            @pl.when(meta_ref[3 * head] > 0)
+            def _(frame=frame, source=source, head=head):
+                by_head(frame, source, head)
 
     def columns(ref, head, low, high, frames):
         if len(frames) == span:
@@ -258,6 +258,7 @@
             all_weights.append(jnp.concatenate(weights, 0).astype(jnp.bfloat16))
         for (start, low, high), weights in zip(all_blocks, all_weights):
             values = columns(vs_ref, head, low, high, frames)
+            values = jnp.concatenate([values, jnp.ones_like(values)], 1)
             sums = jnp.dot(weights, values, preferred_element_type=jnp.float32)
             result = sums[:, :HEAD_DIM] / sums[:, HEAD_DIM:]
             for col in range(start, start + BLOCK_COLS):
@@ -275,9 +276,11 @@
         def _():
             one_head(head, (0.0, 1.0, away), MOST_COLS)
 
-        @pl.when(more_frames & jnp.logical_not(most))
-        def _():
-            one_head(head, (0.0, 1.0, away), MOST_COLS - 1)
+        for fewer in range(MOST_COLS):
+
+            @pl.when(more_frames & (meta_ref[3 * head + 2] == fewer))
+            def _(fewer=fewer):
+                one_head(head, (0.0, 1.0, away), fewer)
 
         @pl.when(jnp.logical_not(more_frames))
         def _():
@@ -303,7 +306,7 @@
         scratch_shapes=[
             pltpu.VMEM((heads, tokens, HEAD_DIM), jnp.bfloat16),
             pltpu.VMEM((heads, 3 * tokens, HEAD_DIM), jnp.bfloat16),
-            pltpu.VMEM((heads, 3 * tokens, 2 * HEAD_DIM), jnp.bfloat16),
+            pltpu.VMEM((heads, 3 * tokens, HEAD_DIM), jnp.bfloat16),
             pltpu.VMEM((lin_rows, HEAD_DIM), jnp.float32),
             pltpu.VMEM(beside.shape, beside.dtype),
             pltpu.SemaphoreType.DMA,

time: 68.3 us -> 68.1 us (level)
  no operation moved by 1% of the time
where the time goes in v5:
time: 68.1 us; the launch traced here: 67.9 us
  blocking collectives  35.8 us (53%)
  starting transfers between devices  14.6 us (21%)
  Pallas kernels  8.64 us (13%)
  waiting for transfers between devices  8.48 us (12%)
    all_to_all x2, blocking collectives, swap(): return lax.all_to_all(slots, 'head', split_axis=0, concat_axis=0)  35.8 us
    ppermute x2, starting transfers between devices, exchange(): return lax.ppermute(array, ('slab', 'head'), both)  10.9 us
    ppermute x2, waiting for transfers between devices, exchange(): return lax.ppermute(array, ('slab', 'head'), both)  8.47 us
    pallas_call x1, Pallas kernels, attend(): pl.pallas_call(functools.partial(attend_kernel, chunk=chunk), out_shape=j...  5.38 us
    all_to_all x1, starting transfers between devices, swap(): return lax.all_to_all(slots, 'head', split_axis=0, concat_axis=0)  3.67 us
    pallas_call x1, Pallas kernels, pack(): pl.pallas_call(pack_kernel, out_shape=(jax.ShapeDtypeStruct((groups, 2 *...  2.37 us
  transfers between devices with their start and end apart: 3, of which 1 were waited for; matrix products, arithmetic and copies ran while one was open for 0% of the time, Pallas kernels for 0%

profile of v5, /device:TPU:16, one launch (start us, length us, event | category | flops | bytes accessed | tf_op | source)
XLA Modules:
  0.0 67.9 jit_solution(15079352646092903399)
XLA Ops:
  0.0 0.0 copy-start
  0.0 2.4 %shard_map.73 = (bf16[8,600,128]{2,1,0:T(8,128)(2,1)S(1)}, bf16[8,104,384]{2,1,0:T(8,128)(2,1)S(1)}) custom-call(s32[1]{0:T(128)} %bitcast.flip_ref, bf16[100,3072]{1,0:T(8,128)(2,1)} %k_ref.1, bf16[100,3072]{1,0:T(8,128)(2,1)} %v_ref.1, bf16[100,3072]{1,0:T(8,128)(2,1)} %q_ref.1, bf16[24,100]{1,0:T(8,128)(2,1)} %bitcast.5, bf16[24,100]{1,0:T(8,128)(2,1)} %bitcast.6, ...), custom_call_target="tpu_custom_call" | custom-call | tf_op jit(solution)/shard_map/pallas_call | solution.py:92
  2.4 0.0 copy-start.1
  2.4 22.4 %all_to_all.15.own_ref = bf16[8,600,128]{2,1,0:T(8,128)(2,1)S(1)} all-to-all(bf16[8,600,128]{2,1,0:T(8,128)(2,1)S(1)} %get-tuple-element.7), channel_id=1, replica_groups=mesh['slab'=64,'head'=8] {'head'}, dimensions={0} | all-to-all | bytes 2457600 | tf_op jit(solution)/shard_map/all_to_all | solution.py:350
  24.8 0.0 copy-done.1
  24.8 9.0 %collective-permute-start = (bf16[8,600,128]{2,1,0:T(8,128)(2,1)S(1)}, bf16[8,600,128]{2,1,0:T(8,128)(2,1)S(1)}, u32[]{:S(2)}, u32[]{:S(2)}) collective-permute-start(bf16[8,600,128]{2,1,0:T(8,128)(2,1)S(1)} %all_to_all.15.own_ref), channel_id=1, source_target_pairs={{8,16},{9,17},{10,18},{11,19},{12,20},{13,21},{14,22},{15,23},{16,... | collective-permute-start | bytes 3686408 | tf_op jit(solution)/shard_map/ppermute | solution.py:346
  33.9 3.7 %all-to-all-start.1 = ((bf16[8,104,384]{2,1,0:T(8,128)(2,1)}), bf16[8,104,384]{2,1,0:T(8,128)(2,1)S(1)}, u32[]{:S(2)}, u32[]{:S(2)}) async-start(bf16[8,104,384]{2,1,0:T(8,128)(2,1)} %copy-done.1), calls=%async_computation.1 | async-start | bytes 1277952 | tf_op jit(solution)/shard_map/all_to_all | solution.py:350
  37.5 0.0 copy-done
  37.5 0.1 constant_dynamic-slice_fusion
  37.6 0.1 copy.8
  37.7 0.1 reshape.13
  37.8 0.1 pad_add_fusion.meta_ref
  37.9 1.9 %collective-permute-start.1 = (bf16[8,600,128]{2,1,0:T(8,128)(2,1)S(1)}, bf16[8,600,128]{2,1,0:T(8,128)(2,1)}, u32[]{:S(2)}, u32[]{:S(2)}) collective-permute-start(bf16[8,600,128]{2,1,0:T(8,128)(2,1)S(1)} %all_to_all.15.own_ref), channel_id=1, source_target_pairs={{0,8},{1,9},{2,10},{3,11},{4,12},{5,13},{6,14},{7,15},{8,0},{9,1},... | collective-permute-start | bytes 3686408 | tf_op jit(solution)/shard_map/ppermute | solution.py:346
  39.8 8.5 %collective-permute-done.array_ref.away_ref = bf16[8,600,128]{2,1,0:T(8,128)(2,1)S(1)} collective-permute-done((bf16[8,600,128]{2,1,0:T(8,128)(2,1)S(1)}, bf16[8,600,128]{2,1,0:T(8,128)(2,1)S(1)}, u32[]{:S(2)}, u32[]{:S(2)}) %collective-permute-start) | collective-permute-done | bytes 1228832 | tf_op jit(solution)/shard_map/ppermute | solution.py:346
  48.3 0.0 all-to-all-done.1.q_ref
  48.3 0.0 collective-permute-done.1.beside_hbm
  48.3 5.4 %shard_map.75 = bf16[8,104,384]{2,1,0:T(8,128)(2,1)S(1)} custom-call(f32[8,128]{1,0:T(8,128)S(1)} %shard_map.74.zeros_ref, s32[10]{0:T(128)S(1)} %pad_add_fusion.meta_ref, bf16[8,104,384]{2,1,0:T(8,128)(2,1)S(1)} %all-to-all-done.1.q_ref, bf16[8,600,128]{2,1,0:T(8,128)(2,1)S(1)} %all_to_all.15.own_ref, ...), custom_call_target="tpu_custom_call" | custom-call | tf_op jit(solution)/shard_map/pallas_call | solution.py:301
  53.7 13.3 %all_to_all.16.in_ref = bf16[8,104,384]{2,1,0:T(8,128)(2,1)S(1)} all-to-all(bf16[8,104,384]{2,1,0:T(8,128)(2,1)S(1)} %shard_map.75), channel_id=1, replica_groups=mesh['slab'=64,'head'=8] {'head'}, dimensions={0} | all-to-all | bytes 1277952 | tf_op jit(solution)/shard_map/all_to_all | solution.py:350
  67.0 0.9 %shard_map.76 = bf16[100,3072]{1,0:T(8,128)(2,1)} custom-call(s32[1]{0:T(128)} %bitcast.flip_ref, bf16[8,104,384]{2,1,0:T(8,128)(2,1)S(1)} %all_to_all.16.in_ref), custom_call_target="tpu_custom_call" | custom-call | tf_op jit(solution)/shard_map/pallas_call | solution.py:119
  (1 shorter events, 0.0 us)
Async XLA Ops:
  0.0 37.5 %copy-start = (s32[24,3]{0,1:T(4,128)S(1)}, s32[24,3]{0,1:T(4,128)}, u32[]{:S(2)}) copy-start(s32[24,3]{0,1:T(4,128)} %param.13) | copy-start | bytes 868
  2.4 22.5 %copy-start.1 = (bf16[8,104,384]{2,1,0:T(8,128)(2,1)}, bf16[8,104,384]{2,1,0:T(8,128)(2,1)S(1)}, u32[]{:S(2)}) copy-start(bf16[8,104,384]{2,1,0:T(8,128)(2,1)S(1)} %get-tuple-element.8) | copy-start | bytes 1916932
  24.8 23.4 %collective-permute-start = (bf16[8,600,128]{2,1,0:T(8,128)(2,1)S(1)}, bf16[8,600,128]{2,1,0:T(8,128)(2,1)S(1)}, u32[]{:S(2)}, u32[]{:S(2)}) collective-permute-start(bf16[8,600,128]{2,1,0:T(8,128)(2,1)S(1)} %all_to_all.15.own_ref), channel_id=1, source_target_pairs={{8,16},{9,17},{10,18},{11,19},{12,20},{13,21},{14,22},{15,23},{16,... | collective-permute-start | bytes 3686408 | tf_op jit(solution)/shard_map/ppermute | solution.py:346
  33.9 14.4 %all-to-all-start.1 = ((bf16[8,104,384]{2,1,0:T(8,128)(2,1)}), bf16[8,104,384]{2,1,0:T(8,128)(2,1)S(1)}, u32[]{:S(2)}, u32[]{:S(2)}) async-start(bf16[8,104,384]{2,1,0:T(8,128)(2,1)} %copy-done.1), calls=%async_computation.1 | async-start | bytes 1277952 | tf_op jit(solution)/shard_map/all_to_all | solution.py:350
  37.9 10.4 %collective-permute-start.1 = (bf16[8,600,128]{2,1,0:T(8,128)(2,1)S(1)}, bf16[8,600,128]{2,1,0:T(8,128)(2,1)}, u32[]{:S(2)}, u32[]{:S(2)}) collective-permute-start(bf16[8,600,128]{2,1,0:T(8,128)(2,1)S(1)} %all_to_all.15.own_ref), channel_id=1, source_target_pairs={{0,8},{1,9},{2,10},{3,11},{4,12},{5,13},{6,14},{7,15},{8,0},{9,1},... | collective-permute-start | bytes 3686408 | tf_op jit(solution)/shard_map/ppermute | solution.py:346

commit v6 on v5

--- a/solution.py
+++ b/solution.py
@@ -106,12 +106,22 @@
     )(flip, *operands)
 
 
-def unpack_kernel(flip_ref, in_ref, out_ref):
+def unpack_kernel(flip_ref, in_ref, out_ref, buf, sems):
     groups, _, width = in_ref.shape
     rows = out_ref.shape[0]
+    copies = []
     for group in range(groups):
         slot = in_ref[group ^ flip_ref[0]]
-        out_ref[:, group * width : (group + 1) * width] = slot[:rows]
+        buf[:, group * width : (group + 1) * width] = slot[:rows]
+        if group % 2 == 1:
+            cols = slice((group - 1) * width, (group + 1) * width)
+            copy = pltpu.make_async_copy(
+                buf.at[:, cols], out_ref.at[:, cols], sems.at[group // 2]
+            )
+            copy.start()
+            copies.append(copy)
+    for copy in copies:
+        copy.wait()
 
 
 def unpack(flip, slots, rows):
@@ -120,7 +130,11 @@
         unpack_kernel,
         out_shape=jax.ShapeDtypeStruct((rows, groups * width), jnp.bfloat16),
         in_specs=[in_smem(), in_vmem()],
-        out_specs=in_vmem(),
+        out_specs=pl.BlockSpec(memory_space=pltpu.HBM),
+        scratch_shapes=[
+            pltpu.VMEM((rows, groups * width), jnp.bfloat16),
+            pltpu.SemaphoreType.DMA((groups // 2,)),
+        ],
         compiler_params=params(4),
     )(flip, slots)
 

time: 68.1 us -> 67.8 us (level)
  Pallas kernels: 8.64 us -> 7.41 us
    pallas_call x1, Pallas kernels: 5.38 us -> 4.17 us  [attend(): pl.pallas_call(functools.partial(attend_kernel, chunk=chunk), out_shape=j...]
where the time goes in v6:
time: 67.8 us; the launch traced here: 67.2 us
  blocking collectives  36.3 us (54%)
  starting transfers between devices  14.6 us (22%)
  waiting for transfers between devices  8.48 us (13%)
  Pallas kernels  7.41 us (11%)
    all_to_all x2, blocking collectives, swap(): return lax.all_to_all(slots, 'head', split_axis=0, concat_axis=0)  36.3 us
    ppermute x2, starting transfers between devices, exchange(): return lax.ppermute(array, ('slab', 'head'), both)  10.9 us
    ppermute x2, waiting for transfers between devices, exchange(): return lax.ppermute(array, ('slab', 'head'), both)  8.47 us
    pallas_call x1, Pallas kernels, attend(): pl.pallas_call(functools.partial(attend_kernel, chunk=chunk), out_shape=j...  4.17 us
    all_to_all x1, starting transfers between devices, swap(): return lax.all_to_all(slots, 'head', split_axis=0, concat_axis=0)  3.67 us
    pallas_call x1, Pallas kernels, pack(): pl.pallas_call(pack_kernel, out_shape=(jax.ShapeDtypeStruct((groups, 2 *...  2.37 us
  transfers between devices with their start and end apart: 3, of which 1 were waited for; matrix products, arithmetic and copies ran while one was open for 0% of the time, Pallas kernels for 0%

profile of v6, /device:TPU:16, one launch (start us, length us, event | category | flops | bytes accessed | tf_op | source)
XLA Modules:
  0.0 67.2 jit_solution(9210552040752454672)
XLA Ops:
  0.0 0.0 copy-start
  0.0 2.4 %shard_map.73 = (bf16[8,600,128]{2,1,0:T(8,128)(2,1)S(1)}, bf16[8,104,384]{2,1,0:T(8,128)(2,1)S(1)}) custom-call(s32[1]{0:T(128)} %bitcast.flip_ref, bf16[100,3072]{1,0:T(8,128)(2,1)} %k_ref.1, bf16[100,3072]{1,0:T(8,128)(2,1)} %v_ref.1, bf16[100,3072]{1,0:T(8,128)(2,1)} %q_ref.1, bf16[24,100]{1,0:T(8,128)(2,1)} %bitcast.5, bf16[24,100]{1,0:T(8,128)(2,1)} %bitcast.6, ...), custom_call_target="tpu_custom_call" | custom-call | tf_op jit(solution)/shard_map/pallas_call | solution.py:92
  2.4 0.0 copy-start.1
  2.4 22.4 %all_to_all.15.own_ref = bf16[8,600,128]{2,1,0:T(8,128)(2,1)S(1)} all-to-all(bf16[8,600,128]{2,1,0:T(8,128)(2,1)S(1)} %get-tuple-element.7), channel_id=1, replica_groups=mesh['slab'=64,'head'=8] {'head'}, dimensions={0} | all-to-all | bytes 2457600 | tf_op jit(solution)/shard_map/all_to_all | solution.py:364
  24.8 0.0 copy-done.1
  24.8 9.0 %collective-permute-start = (bf16[8,600,128]{2,1,0:T(8,128)(2,1)S(1)}, bf16[8,600,128]{2,1,0:T(8,128)(2,1)S(1)}, u32[]{:S(2)}, u32[]{:S(2)}) collective-permute-start(bf16[8,600,128]{2,1,0:T(8,128)(2,1)S(1)} %all_to_all.15.own_ref), channel_id=1, source_target_pairs={{8,16},{9,17},{10,18},{11,19},{12,20},{13,21},{14,22},{15,23},{16,... | collective-permute-start | bytes 3686408 | tf_op jit(solution)/shard_map/ppermute | solution.py:360
  33.9 3.7 %all-to-all-start.1 = ((bf16[8,104,384]{2,1,0:T(8,128)(2,1)}), bf16[8,104,384]{2,1,0:T(8,128)(2,1)S(1)}, u32[]{:S(2)}, u32[]{:S(2)}) async-start(bf16[8,104,384]{2,1,0:T(8,128)(2,1)} %copy-done.1), calls=%async_computation.1 | async-start | bytes 1277952 | tf_op jit(solution)/shard_map/all_to_all | solution.py:364
  37.5 0.0 copy-done
  37.5 0.1 constant_dynamic-slice_fusion
  37.6 0.1 copy.8
  37.7 0.1 reshape.13
  37.8 0.1 pad_add_fusion.meta_ref
  37.9 1.9 %collective-permute-start.1 = (bf16[8,600,128]{2,1,0:T(8,128)(2,1)S(1)}, bf16[8,600,128]{2,1,0:T(8,128)(2,1)}, u32[]{:S(2)}, u32[]{:S(2)}) collective-permute-start(bf16[8,600,128]{2,1,0:T(8,128)(2,1)S(1)} %all_to_all.15.own_ref), channel_id=1, source_target_pairs={{0,8},{1,9},{2,10},{3,11},{4,12},{5,13},{6,14},{7,15},{8,0},{9,1},... | collective-permute-start | bytes 3686408 | tf_op jit(solution)/shard_map/ppermute | solution.py:360
  39.8 8.5 %collective-permute-done.array_ref.away_ref = bf16[8,600,128]{2,1,0:T(8,128)(2,1)S(1)} collective-permute-done((bf16[8,600,128]{2,1,0:T(8,128)(2,1)S(1)}, bf16[8,600,128]{2,1,0:T(8,128)(2,1)S(1)}, u32[]{:S(2)}, u32[]{:S(2)}) %collective-permute-start) | collective-permute-done | bytes 1228832 | tf_op jit(solution)/shard_map/ppermute | solution.py:360
  48.3 0.0 all-to-all-done.1.q_ref
  48.3 0.0 collective-permute-done.1.beside_hbm
  48.3 4.2 %shard_map.75 = bf16[8,104,384]{2,1,0:T(8,128)(2,1)S(1)} custom-call(f32[8,128]{1,0:T(8,128)S(1)} %shard_map.74.zeros_ref, s32[10]{0:T(128)S(1)} %pad_add_fusion.meta_ref, bf16[8,104,384]{2,1,0:T(8,128)(2,1)S(1)} %all-to-all-done.1.q_ref, bf16[8,600,128]{2,1,0:T(8,128)(2,1)S(1)} %all_to_all.15.own_ref, ...), custom_call_target="tpu_custom_call" | custom-call | tf_op jit(solution)/shard_map/pallas_call | solution.py:315
  52.5 13.9 %all_to_all.16.in_ref = bf16[8,104,384]{2,1,0:T(8,128)(2,1)S(1)} all-to-all(bf16[8,104,384]{2,1,0:T(8,128)(2,1)S(1)} %shard_map.75), channel_id=1, replica_groups=mesh['slab'=64,'head'=8] {'head'}, dimensions={0} | all-to-all | bytes 1277952 | tf_op jit(solution)/shard_map/all_to_all | solution.py:364
  66.3 0.9 %shard_map.76 = bf16[100,3072]{1,0:T(8,128)(2,1)} custom-call(s32[1]{0:T(128)} %bitcast.flip_ref, bf16[8,104,384]{2,1,0:T(8,128)(2,1)S(1)} %all_to_all.16.in_ref), custom_call_target="tpu_custom_call" | custom-call | tf_op jit(solution)/shard_map/pallas_call | solution.py:129
  (1 shorter events, 0.0 us)
Async XLA Ops:
  0.0 37.5 %copy-start = (s32[24,3]{0,1:T(4,128)S(1)}, s32[24,3]{0,1:T(4,128)}, u32[]{:S(2)}) copy-start(s32[24,3]{0,1:T(4,128)} %param.13) | copy-start | bytes 868
  2.4 22.5 %copy-start.1 = (bf16[8,104,384]{2,1,0:T(8,128)(2,1)}, bf16[8,104,384]{2,1,0:T(8,128)(2,1)S(1)}, u32[]{:S(2)}) copy-start(bf16[8,104,384]{2,1,0:T(8,128)(2,1)S(1)} %get-tuple-element.8) | copy-start | bytes 1916932
  24.8 23.4 %collective-permute-start = (bf16[8,600,128]{2,1,0:T(8,128)(2,1)S(1)}, bf16[8,600,128]{2,1,0:T(8,128)(2,1)S(1)}, u32[]{:S(2)}, u32[]{:S(2)}) collective-permute-start(bf16[8,600,128]{2,1,0:T(8,128)(2,1)S(1)} %all_to_all.15.own_ref), channel_id=1, source_target_pairs={{8,16},{9,17},{10,18},{11,19},{12,20},{13,21},{14,22},{15,23},{16,... | collective-permute-start | bytes 3686408 | tf_op jit(solution)/shard_map/ppermute | solution.py:360
  33.9 14.4 %all-to-all-start.1 = ((bf16[8,104,384]{2,1,0:T(8,128)(2,1)}), bf16[8,104,384]{2,1,0:T(8,128)(2,1)S(1)}, u32[]{:S(2)}, u32[]{:S(2)}) async-start(bf16[8,104,384]{2,1,0:T(8,128)(2,1)} %copy-done.1), calls=%async_computation.1 | async-start | bytes 1277952 | tf_op jit(solution)/shard_map/all_to_all | solution.py:364
  37.9 10.4 %collective-permute-start.1 = (bf16[8,600,128]{2,1,0:T(8,128)(2,1)S(1)}, bf16[8,600,128]{2,1,0:T(8,128)(2,1)}, u32[]{:S(2)}, u32[]{:S(2)}) collective-permute-start(bf16[8,600,128]{2,1,0:T(8,128)(2,1)S(1)} %all_to_all.15.own_ref), channel_id=1, source_target_pairs={{0,8},{1,9},{2,10},{3,11},{4,12},{5,13},{6,14},{7,15},{8,0},{9,1},... | collective-permute-start | bytes 3686408 | tf_op jit(solution)/shard_map/ppermute | solution.py:360
